TPU v7x, 512 devices: a whole 4x4x16 slice. The times are simulated.
512 devices in a mesh: user: 64 (over z, y), item: 8 (over x, core).
Axes of the slice: x: 4, y: 4, z: 16, core: 2. Of those that a mesh axis runs over, the one named last changes fastest.
Arguments:
- candidates: bfloat16 [1024, 128, 512], P(('user', 'item')), may hold values from -6 to 6
- proj_weight: bfloat16 [512, 2048], P('user'), may hold values from -0.25 to 0.25
- out_weight: bfloat16 [512, 512], P('user'), may hold values from -0.25 to 0.25
- history_kv: bfloat16 [1024, 4, 64, 1024], P('item', None, 'user'), may hold values from -6 to 6
- scorer_user: int32 [1024], replicated, may hold values from 0 to 1023, as said below
- hist_len: int32 [1024], P(('user', 'item')), may hold values from 16 to 256, as said below
- cand_item: int32 [1024, 128], P(('user', 'item')), may hold values from 0 to 8191, as said below
- item_table: bfloat16 [8192, 512], P('item'), may hold values from -0.25 to 0.25
Outputs:
- logits: float32 [1024, 128], P(('user', 'item'))
Inputs may be any that keep to these rules, and one draw needn't show every extreme that they name: `scorer_user`: A permutation of all users; scorer slot s lies on the device at position s // 2 of the flattened user, item axes, and its user lies in owner block (s // 2) % 8 of 128 users. `hist_len`: some slot has length 256. `cand_item`: item id // 1024 is the item shard holding its row. In the rows of one device no shard is named by more than 96 rows, and in every draw one shard is named by exactly 96 rows of every device.
All inputs are finite; a program needn't handle non-finite values.
Results may differ from a plain program's by a relative error of at most 0.0075.
Values may be sent and summed in bfloat16 or wider, within the bound.
No kernel may reach another device: no remote copies, remote signals or barrier semaphores. Data moves between devices by JAX's collectives and lax.ppermute only.
A program may use at most 64 MiB of HBM per device.

v0:
```python
import jax
import jax.numpy as jnp
from jax import lax
from jax.sharding import PartitionSpec as P

HEADS = 4


def layer_norm(values):
    center = values - jnp.mean(values, axis=-1, keepdims=True)
    spread = jnp.mean(center * center, axis=-1, keepdims=True)
    return center * lax.rsqrt(spread + 1e-06)


def body(
    candidates, proj_weight, out_weight, history_kv, scorer_user, hist_len, cand_item, item_table
):
    user_count, cand_count, model_width = candidates.shape
    row_count = user_count * cand_count
    head_count = HEADS
    head_size = model_width // head_count
    cand_rows = candidates.reshape(row_count, model_width)
    normed = layer_norm(cand_rows.astype(jnp.float32)).astype(jnp.bfloat16)
    columns = normed
    proj = jnp.dot(
        columns,
        lax.all_gather(proj_weight, "user", axis=0, tiled=True),
        preferred_element_type=jnp.float32,
    )
    proj = jax.nn.silu(proj)
    gate_u = proj[:, :model_width]
    cand_v = (
        proj[:, model_width : 2 * model_width]
        .astype(jnp.bfloat16)
        .reshape(user_count, cand_count, head_count, head_size)
    )
    cand_q = (
        proj[:, 2 * model_width : 3 * model_width]
        .astype(jnp.bfloat16)
        .reshape(user_count, cand_count, head_count, head_size)
    )
    cand_k = (
        proj[:, 3 * model_width :]
        .astype(jnp.bfloat16)
        .reshape(user_count, cand_count, head_count, head_size)
    )
    owner_count = lax.axis_size("user")
    shard_count = lax.axis_size("item")
    item_index = lax.axis_index("item")
    group_users = history_kv.shape[0]
    slot_table = scorer_user.reshape(owner_count, shard_count, user_count)
    mine = lax.dynamic_index_in_dim(slot_table, item_index, axis=1, keepdims=False)
    local_ids = jnp.transpose(mine - item_index * group_users)
    picked = jnp.take(history_kv, local_ids, axis=0)
    arrived = lax.all_to_all(picked, "user", split_axis=1, concat_axis=3, tiled=True)
    history = arrived.reshape(user_count, -1, 2 * model_width)
    positions = history.shape[1]
    hist_keys = history[:, :, :model_width].reshape(user_count, positions, head_count, head_size)
    hist_values = history[:, :, model_width:].reshape(user_count, positions, head_count, head_size)
    score_scale = head_size ** (-0.5)
    scores = (
        jnp.einsum("uchx,uphx->uhcp", cand_q, hist_keys, preferred_element_type=jnp.float32)
        * score_scale
    )
    live_mask = jnp.arange(positions)[None, :] < hist_len[:, None]
    hist_w = jnp.where(live_mask[:, None, None, :], jax.nn.silu(scores), 0.0).astype(jnp.bfloat16)
    attention = jnp.einsum(
        "uhcp,uphx->uchx", hist_w, hist_values, preferred_element_type=jnp.float32
    )
    self_score = (
        jnp.sum(cand_q.astype(jnp.float32) * cand_k.astype(jnp.float32), axis=-1) * score_scale
    )
    self_w = jax.nn.silu(self_score).astype(jnp.bfloat16)
    attention = attention + self_w.astype(jnp.float32)[..., None] * cand_v.astype(jnp.float32)
    attended = attention / (hist_len.astype(jnp.float32) + 1.0)[:, None, None, None]
    attended = attended.reshape(row_count, model_width)
    gated = (layer_norm(attended) * gate_u).astype(jnp.bfloat16)
    columns = gated
    update = jnp.dot(
        columns,
        lax.all_gather(out_weight, "user", axis=0, tiled=True),
        preferred_element_type=jnp.float32,
    )
    final = cand_rows.astype(jnp.float32) + update
    unit = (final * lax.rsqrt(jnp.mean(final * final, axis=-1, keepdims=True) + 1e-06)).astype(
        jnp.bfloat16
    )
    item_ids = cand_item.reshape(row_count)
    item_rows = item_table.shape[0]
    item_shard = item_ids // item_rows
    one_hot = (item_shard[:, None] == jnp.arange(shard_count)[None, :]).astype(jnp.int32)
    slot_rank = jnp.sum((jnp.cumsum(one_hot, axis=0) - one_hot) * one_hot, axis=1)
    capacity = row_count // 4 + row_count // shard_count
    slot_index = item_shard * capacity + slot_rank
    source_rows = (
        jnp.zeros((shard_count * capacity,), jnp.int32)
        .at[slot_index]
        .set(jnp.arange(row_count, dtype=jnp.int32))
    )
    send_rows = jnp.take(unit, source_rows, axis=0).reshape(shard_count, capacity, model_width)
    send_ids = (
        jnp.zeros((shard_count * capacity,), jnp.int32).at[slot_index].set(item_ids % item_rows)
    )
    send_ids = send_ids.reshape(shard_count, capacity)
    got_rows = lax.all_to_all(send_rows, "item", split_axis=0, concat_axis=0, tiled=True)
    got_ids = lax.all_to_all(send_ids, "item", split_axis=0, concat_axis=0, tiled=True)
    fetched = jnp.take(item_table, got_ids, axis=0)
    scored = jnp.sum(got_rows.astype(jnp.float32) * fetched.astype(jnp.float32), axis=-1)
    returned = lax.all_to_all(scored, "item", split_axis=0, concat_axis=0, tiled=True)
    logits = returned.reshape(-1)[slot_index]
    return logits.reshape(user_count, cand_count)


def solution(mesh):
    return jax.shard_map(
        body,
        mesh=mesh,
        in_specs=(
            P(("user", "item"), None, None),
            P("user", None),
            P("user", None),
            P("item", None, "user", None),
            P(),
            P(("user", "item")),
            P(("user", "item"), None),
            P("item", None),
        ),
        out_specs=P(("user", "item"), None),
        check_vma=False,
    )
```

profile of v0, /device:TPU:1, one launch (start us, length us, event | category | flops | bytes accessed | tf_op | source)
XLA Modules:
  0.0 240.7 jit_solution(5203106031074406644)
XLA Ops:
  6.5 0.7 all-gather.2.cloned.1.call-update
  7.3 0.9 reshape.324
  8.4 1.5 gather_fusion
  10.4 2.1 copy.50
  12.4 19.4 %all-to-all-start = ((bf16[2,64,4,1,1024]{4,0,2,3,1:T(2,128)(2,1)}), bf16[2,64,4,1,1024]{4,0,2,3,1:T(2,128)(2,1)S(1)}, u32[]{:S(2)}, u32[]{:S(2)}) async-start(bf16[2,64,4,1,1024]{4,0,2,3,1:T(2,128)(2,1)} %copy.50), calls=%async_computation | async-start | bytes 2097152 | tf_op jit(solution)/shard_map/all_to_all | solution.py:55
  32.9 1.4 scatter_custom_fusion
  34.4 1.4 scatter_custom_fusion.1
  35.8 0.7 all_to_all.34
  36.6 116.9 %all_gather.7 = bf16[512,512]{1,0:T(8,128)(2,1)S(1)} all-gather(bf16[8,512]{1,0:T(8,128)(2,1)S(1)} %copy-done.5), channel_id=1, replica_groups=mesh['user'=64,'item'=8] {'user'}, dimensions={0}, use_global_device_ids=true | all-gather | bytes 532480 | tf_op jit(solution)/shard_map/all_gather | solution.py:81
  154.4 2.9 %all-gather.2.cloned.1.call-done = bf16[512,2048]{1,0:T(8,128)(2,1)} async-done(((bf16[8,2048]{1,0:T(8,128)(2,1)}), bf16[512,2048]{1,0:T(8,128)(2,1)}) %all-gather.2.cloned.1.call-update) | async-done | bytes 2097168 | tf_op jit(solution)/shard_map/all_gather | solution.py:27
  157.3 3.8 %fusion.30 = (bf16[256,2048]{1,0:T(8,128)(2,1)S(1)}, f32[256,2048]{1,0:T(8,128)}) fusion(bf16[256,512]{1,0:T(8,128)(2,1)S(1)} %fusion.6, bf16[512,2048]{1,0:T(8,128)(2,1)} %all-gather.2.cloned.1.call-done), kind=kOutput, calls=%fused_computation.93 | convolution fusion | flops 539492352 | bytes 5505024 | tf_op jit(solution)/shard_map/dot_general | solution.py:25
  161.1 1.1 slice_convert_fusion.1
  162.2 1.2 reshape.334
  163.4 1.0 copy.57
  164.4 1.2 reshape.333
  165.6 1.7 reshape.327
  167.3 1.3 multiply_reduce_fusion.3
  168.7 23.3 %all-to-all-start.2 = ((s32[8,1,96]{2,1,0:T(1,128)}), s32[8,1,96]{2,1,0:T(1,128)S(1)}, u32[]{:S(2)}, u32[]{:S(2)}) async-start(s32[8,1,96]{2,1,0:T(1,128)} %all_to_all.34), calls=%async_computation.2 | async-start | bytes 8192 | tf_op jit(solution)/shard_map/all_to_all | solution.py:106
  192.7 1.0 copy.52
  193.7 1.0 copy.53
  194.7 2.1 fusion.32
  197.1 1.5 multiply_reduce_fusion.1
  198.8 2.7 %gather_fusion.1 = bf16[768,512]{1,0:T(8,128)(2,1)S(1)} fusion(bf16[256,512]{1,0:T(8,128)(2,1)S(1)} %multiply_convert_fusion, s32[1024]{0:T(1024)S(1)} %pad_clamp_fusion.2), kind=kCustom, calls=%fused_computation.1 | custom fusion | bytes 1575936 | tf_op jit(solution)/shard_map/jit(_take)/gather | solution.py:100
  201.5 1.1 broadcast_select_fusion.1
  202.5 4.8 %all-to-all-start.1 = ((bf16[8,96,512]{2,1,0:T(8,128)(2,1)}), bf16[8,96,512]{2,1,0:T(8,128)(2,1)}, u32[]{:S(2)}, u32[]{:S(2)}) async-start(bf16[8,96,512]{2,1,0:T(8,128)(2,1)} %broadcast_select_fusion.1), calls=%async_computation.1 | async-start | bytes 1572864 | tf_op jit(solution)/shard_map/all_to_all | solution.py:105
  207.4 2.7 %gather_fusion.2 = bf16[768,512]{1,0:T(8,128)(2,1)S(1)} fusion(bf16[1024,512]{1,0:T(8,128)(2,1)S(1)} %copy-done.1, s32[1024]{0:T(1024)S(1)} %pad_clamp_fusion.1), kind=kCustom, calls=%fused_computation.2 | custom fusion | bytes 1575936 | tf_op jit(solution)/shard_map/jit(_take)/gather | solution.py:107
  210.1 9.6 %all-to-all-done.1 = bf16[8,96,512]{2,1,0:T(8,128)(2,1)} async-done(((bf16[8,96,512]{2,1,0:T(8,128)(2,1)}), bf16[8,96,512]{2,1,0:T(8,128)(2,1)}, u32[]{:S(2)}, u32[]{:S(2)}) %all-to-all-start.1) | async-done | bytes 786464 | tf_op jit(solution)/shard_map/all_to_all | solution.py:105
  219.7 2.2 multiply_reduce_fusion
  221.9 4.1 %all-to-all-start.3 = ((f32[8,1,96]{2,1,0:T(1,128)}), f32[8,1,96]{2,1,0:T(1,128)S(1)}, u32[]{:S(2)}, u32[]{:S(2)}) async-start(f32[8,1,96]{2,1,0:T(1,128)} %bitcast.28), calls=%async_computation.3 | async-start | bytes 8192 | tf_op jit(solution)/shard_map/all_to_all | solution.py:109
  226.1 4.6 %all-to-all-done.3 = f32[8,1,96]{2,1,0:T(1,128)S(1)} async-done(((f32[8,1,96]{2,1,0:T(1,128)}), f32[8,1,96]{2,1,0:T(1,128)S(1)}, u32[]{:S(2)}, u32[]{:S(2)}) %all-to-all-start.3) | async-done | bytes 3104 | tf_op jit(solution)/shard_map/all_to_all | solution.py:109
  231.1 0.7 reduce.9
  231.9 1.9 gather_fusion.3
  (64 shorter events, 4.8 us)
Async XLA Ops:
  6.5 1.8 copy-start
  6.5 150.8 %all-gather.2.cloned.1.call-start = ((), (), s32[]{:S(2)}) async-start(), calls=%async_computation.4 | async-start | bytes 2129920 | tf_op jit(solution)/shard_map/all_gather | solution.py:27
  10.3 21.5 %copy-start.4 = (s32[2,128]{1,0:T(2,128)S(1)}, s32[2,128]{1,0:T(2,128)}, u32[]{:S(2)}) copy-start(s32[2,128]{1,0:T(2,128)} %param.14) | copy-start | bytes 3076
  10.3 26.1 %copy-start.2 = (bf16[2,128,512]{2,1,0:T(8,128)(2,1)S(1)}, bf16[2,128,512]{2,1,0:T(8,128)(2,1)}, u32[]{:S(2)}) copy-start(bf16[2,128,512]{2,1,0:T(8,128)(2,1)} %param.8) | copy-start | bytes 786436
  10.3 26.2 %copy-start.5 = (bf16[8,512]{1,0:T(8,128)(2,1)S(1)}, bf16[8,512]{1,0:T(8,128)(2,1)}, u32[]{:S(2)}) copy-start(bf16[8,512]{1,0:T(8,128)(2,1)} %param.10) | copy-start | bytes 24580
  12.4 141.3 %copy-start.6 = (s32[2]{0:T(128)S(1)}, s32[2]{0:T(128)}, u32[]{:S(2)}) copy-start(s32[2]{0:T(128)} %param.13) | copy-start | bytes 28
  12.4 156.3 %all-to-all-start = ((bf16[2,64,4,1,1024]{4,0,2,3,1:T(2,128)(2,1)}), bf16[2,64,4,1,1024]{4,0,2,3,1:T(2,128)(2,1)S(1)}, u32[]{:S(2)}, u32[]{:S(2)}) async-start(bf16[2,64,4,1,1024]{4,0,2,3,1:T(2,128)(2,1)} %copy.50), calls=%async_computation | async-start | bytes 2097152 | tf_op jit(solution)/shard_map/all_to_all | solution.py:55
  168.7 33.8 %all-to-all-start.2 = ((s32[8,1,96]{2,1,0:T(1,128)}), s32[8,1,96]{2,1,0:T(1,128)S(1)}, u32[]{:S(2)}, u32[]{:S(2)}) async-start(s32[8,1,96]{2,1,0:T(1,128)} %all_to_all.34), calls=%async_computation.2 | async-start | bytes 8192 | tf_op jit(solution)/shard_map/all_to_all | solution.py:106
  192.6 2.1 copy-start.3
  192.6 2.1 copy-start.7
  201.4 6.0 %copy-start.1 = (bf16[1024,512]{1,0:T(8,128)(2,1)S(1)}, bf16[1024,512]{1,0:T(8,128)(2,1)}, u32[]{:S(2)}) copy-start(bf16[1024,512]{1,0:T(8,128)(2,1)} %param.15) | copy-start | bytes 3145732
  202.5 17.2 %all-to-all-start.1 = ((bf16[8,96,512]{2,1,0:T(8,128)(2,1)}), bf16[8,96,512]{2,1,0:T(8,128)(2,1)}, u32[]{:S(2)}, u32[]{:S(2)}) async-start(bf16[8,96,512]{2,1,0:T(8,128)(2,1)} %broadcast_select_fusion.1), calls=%async_computation.1 | async-start | bytes 1572864 | tf_op jit(solution)/shard_map/all_to_all | solution.py:105
  221.9 8.7 %all-to-all-start.3 = ((f32[8,1,96]{2,1,0:T(1,128)}), f32[8,1,96]{2,1,0:T(1,128)S(1)}, u32[]{:S(2)}, u32[]{:S(2)}) async-start(f32[8,1,96]{2,1,0:T(1,128)} %bitcast.28), calls=%async_computation.3 | async-start | bytes 8192 | tf_op jit(solution)/shard_map/all_to_all | solution.py:109
Sparse Core Ops, SparseCore 0:
  10.3 146.9 all-gather.1
where the time goes:
time: 241 us
  blocking collectives  117 us (49%)
  starting transfers between devices  51.6 us (21%)
  local copies, waits for them, and re-layouts  24.8 us (10%)
  waiting for transfers between devices  17.8 us (7%)
  between operations  13.7 us (6%)
  other arithmetic  8.64 us (4%)
  matrix products  7.3 us (3%)
    all_gather x1, blocking collectives, body(): lax.all_gather(out_weight, 'user', axis=0, tiled=True)  117 us
    all_to_all x1, starting transfers between devices, body(): lax.all_to_all(send_ids, 'item', split_axis=0, concat_axis=0, tiled=True)  23.3 us
    all_to_all x1, starting transfers between devices, body(): lax.all_to_all(picked, 'user', split_axis=1, concat_axis=3, tiled=True)  19.4 us
    all_to_all x1, waiting for transfers between devices, body(): lax.all_to_all(send_rows, 'item', split_axis=0, concat_axis=0, tiled=True)  9.6 us
  transfers between devices with their start and end apart: 5, of which 3 were waited for; matrix products, arithmetic and copies ran while one was open for 14% of the time, Pallas kernels for 0%

commit v1 on v0

v1 whole, which is shorter than its diff:
```python
import functools

import jax
import jax.numpy as jnp
from jax import lax
from jax.experimental import pallas as pl
from jax.experimental.pallas import tpu as pltpu
from jax.sharding import Mesh, PartitionSpec as P

HEADS = 4
CAP = 96
F32 = jnp.float32
BF16 = jnp.bfloat16
VMEM = pltpu.VMEM
SMEM = pltpu.SMEM
VMEM_LIMIT = 40 * 1024 * 1024

USER = ("z", "y")
ITEM = ("x", "core")


def params():
    return pltpu.CompilerParams(vmem_limit_bytes=VMEM_LIMIT)


def silu(values):
    return values * jax.nn.sigmoid(values)


def iota(shape, dim):
    return lax.broadcasted_iota(jnp.int32, shape, dim)


def dot(a, b):
    return jnp.dot(a, b, preferred_element_type=F32)


def spread_kernel(place, proj_weight, out_weight, out):
    item = place[0]
    chosen = iota((proj_weight.shape[0], 1), 0) == item
    wide = jnp.where(chosen, proj_weight[...].astype(F32), 0.0)
    narrow = jnp.where(chosen, out_weight[...].astype(F32), 0.0)
    row = jnp.concatenate(
        [jnp.sum(wide, axis=0, keepdims=True), jnp.sum(narrow, axis=0, keepdims=True)], axis=1
    )
    half = row.shape[1] // 2
    pair = jnp.concatenate([row[:, :half], row[:, half:]], axis=0).astype(BF16)
    for k in range(out.shape[0]):
        out[k] = pair


def spread(place, proj_weight, out_weight, copies):
    columns = proj_weight.shape[1] + out_weight.shape[1]
    return pl.pallas_call(
        spread_kernel,
        out_shape=jax.ShapeDtypeStruct((copies, 2, columns // 2), BF16),
        in_specs=[pl.BlockSpec(memory_space=SMEM)] + [pl.BlockSpec(memory_space=VMEM)] * 2,
        out_specs=pl.BlockSpec(memory_space=VMEM),
        compiler_params=params(),
        name="spread_weight_row",
    )(place, proj_weight, out_weight)


def block_kernel(first, rows, out):
    whole = jnp.concatenate([rows[:, 0, :], rows[:, 1, :]], axis=1)
    peers, width = whole.shape[0], out.shape[1]
    for k in range(whole.shape[1] // width):
        out[k * peers : (k + 1) * peers, :] = whole[:, k * width : (k + 1) * width]


def block(first, rows, width):
    peers, _, half = rows.shape
    return pl.pallas_call(
        block_kernel,
        out_shape=jax.ShapeDtypeStruct((peers * 2 * half // width, width), BF16),
        in_specs=[pl.BlockSpec(memory_space=pl.ANY), pl.BlockSpec(memory_space=VMEM)],
        out_specs=pl.BlockSpec(memory_space=VMEM),
        compiler_params=params(),
        name="block_weight_rows",
    )(first, rows)


def pick_kernel(slots, place, hist, first, out):
    item = place[0]
    owners = out.shape[0]
    users = out.shape[1]
    group = hist.shape[0]

    def one(owner, carry):
        for slot in range(users):
            local = slots[(owner * 8 + item) * users + slot] - item * group
            out[owner, slot] = hist[local]
        return carry

    lax.fori_loop(0, owners, one, 0, unroll=4)


def pick(scorer_user, place, hist, first, owners, users):
    return pl.pallas_call(
        pick_kernel,
        out_shape=jax.ShapeDtypeStruct((owners, users) + hist.shape[1:], hist.dtype),
        in_specs=[
            pl.BlockSpec(memory_space=SMEM),
            pl.BlockSpec(memory_space=SMEM),
            pl.BlockSpec(memory_space=VMEM),
            pl.BlockSpec(memory_space=pl.ANY),
        ],
        out_specs=pl.BlockSpec(memory_space=VMEM),
        compiler_params=params(),
        name="pick_history",
    )(scorer_user, place, hist, first)


def fetch_kernel(place, ids, table, out):
    item = place[0]
    x, core = place[1], place[2]
    rows = table.shape[0]
    count = ids.shape[1]
    before = (iota((count, count), 0) < iota((count, count), 1)).astype(BF16)
    all_ids = ids[...]
    mine = (all_ids // rows == item)
    mine_f = mine.astype(F32)
    rank = dot(mine.astype(BF16), before)
    key = jnp.where(mine, rank, -1.0)
    local = (all_ids % rows).astype(F32)
    tab = table[...]
    peer_of = iota((ids.shape[0], 1), 0)
    for k in range(8):
        peer = ((x + k // 2) % 4) * 2 + (core + k % 2) % 2
        choose = (peer_of == peer).astype(F32)
        key_k = jnp.sum((key + 1.0) * choose, axis=0, keepdims=True) - 1.0
        local_k = jnp.sum(local * choose, axis=0, keepdims=True)
        slot = iota((CAP, count), 0).astype(F32)
        row_of = jnp.sum(jnp.where(slot == key_k, local_k, 0.0), axis=1, keepdims=True)
        hot = (iota((CAP, rows), 1).astype(F32) == row_of).astype(BF16)
        out[k // 2, k % 2] = dot(hot, tab).astype(BF16)


def fetch(place, ids, table):
    return pl.pallas_call(
        fetch_kernel,
        out_shape=jax.ShapeDtypeStruct((4, 2, CAP, table.shape[1]), table.dtype),
        in_specs=[
            pl.BlockSpec(memory_space=SMEM),
            pl.BlockSpec(memory_space=VMEM),
            pl.BlockSpec(memory_space=VMEM),
        ],
        out_specs=pl.BlockSpec(memory_space=VMEM),
        compiler_params=params(),
        name="fetch_rows",
    )(place, ids, table)


def pack_x_kernel(found, weight, *outs):
    for k, out in enumerate(outs):
        out[:CAP] = found[k, 0]
        out[CAP:-CAP] = weight[...]
        out[-CAP:] = found[k, 1]


def pack_x(found, weight):
    rows = weight.shape[0] + 2 * CAP
    return pl.pallas_call(
        pack_x_kernel,
        out_shape=(jax.ShapeDtypeStruct((rows, weight.shape[1]), BF16),) * 4,
        in_specs=[pl.BlockSpec(memory_space=VMEM)] * 2,
        out_specs=(pl.BlockSpec(memory_space=VMEM),) * 4,
        compiler_params=params(),
        name="pack_for_x",
    )(found, weight)


def pack_core_kernel(*refs):
    out = refs[-1]
    for k, ref in enumerate(refs[:-1]):
        out[k] = ref[CAP:]


def pack_core(pieces):
    rows, width = pieces[0].shape
    return pl.pallas_call(
        pack_core_kernel,
        out_shape=jax.ShapeDtypeStruct((4, rows - CAP, width), BF16),
        in_specs=[pl.BlockSpec(memory_space=VMEM)] * 4,
        out_specs=pl.BlockSpec(memory_space=VMEM),
        compiler_params=params(),
        name="pack_for_core",
    )(*pieces)


def proj_kernel(
    place, ids, cand, p0, p1, p2, p3, other, rows_out, gate, query, self_term, out_weight
):
    own = (p0, p1, p2, p3)
    x, core = place[1], place[2]
    rows, width = cand.shape
    values = cand[...].astype(F32)
    center = values - jnp.mean(values, axis=-1, keepdims=True)
    spread = jnp.mean(center * center, axis=-1, keepdims=True)
    normed = (center * lax.rsqrt(spread + 1e-06)).astype(BF16)
    g = iota((width, width), 1)
    from_x = (x + 4 - (g // 64) % 4) % 4
    from_core = (core + g // 256) % 2
    natural = (g % 16) * 32 + ((g // 16) % 4) * 8 + from_x * 2 + from_core
    perm = (iota((width, width), 0) == natural).astype(BF16)
    normed = dot(normed, perm).astype(BF16)

    def weight(cols):
        parts = []
        for y in range(4):
            at = (y * 5 + cols) * 16
            parts.append(at)
        blocks = [own[k][CAP + at : CAP + at + 16] for k in range(4) for at in parts]
        blocks += [other[k, at : at + 16] for k in range(4) for at in parts]
        return jnp.concatenate(blocks, axis=0)

    out_weight[...] = dot(perm, weight(4)).astype(BF16)
    gate[...] = silu(dot(normed, weight(0)))
    value = silu(dot(normed, weight(1))).astype(BF16).astype(F32)
    q = silu(dot(normed, weight(2))).astype(BF16)
    k = silu(dot(normed, weight(3))).astype(BF16)
    query[...] = q
    product = q.astype(F32) * k.astype(F32)
    head = width // HEADS
    for h in range(HEADS):
        cols = slice(h * head, (h + 1) * head)
        score = jnp.sum(product[:, cols], axis=-1, keepdims=True) * head ** (-0.5)
        self_term[:, cols] = silu(score).astype(BF16).astype(F32) * value[:, cols]

    shard = ids[...] // 1024
    before = (iota((rows, rows), 0) < iota((rows, rows), 1)).astype(BF16)
    hot = iota((8, rows), 0) == shard
    ranks = dot(hot.astype(BF16), before)
    rank = jnp.sum(jnp.where(hot, ranks, 0.0), axis=0, keepdims=True)
    offset = ((x + 4 - shard // 2) % 4) * 2 + (core + 2 - shard % 2) % 2
    total = jnp.zeros((rows, width), F32)
    for j in range(8):
        key = jnp.where(offset == j, rank, -1.0)
        chosen = (iota((CAP, rows), 0).astype(F32) == key).astype(BF16)
        piece = other[j // 2, -CAP:] if j % 2 else own[j // 2][:CAP]
        total += lax.dot_general(
            chosen, piece, (((0,), (0,)), ((), ())), preferred_element_type=F32
        )
    rows_out[...] = total.astype(BF16)


def project(place, ids, cand, pieces, other):
    rows, width = cand.shape
    return pl.pallas_call(
        proj_kernel,
        out_shape=(
            jax.ShapeDtypeStruct((rows, width), BF16),
            jax.ShapeDtypeStruct((rows, width), F32),
            jax.ShapeDtypeStruct((rows, width), BF16),
            jax.ShapeDtypeStruct((rows, width), F32),
            jax.ShapeDtypeStruct((width, width), BF16),
        ),
        in_specs=[pl.BlockSpec(memory_space=SMEM)] + [pl.BlockSpec(memory_space=VMEM)] * 7,
        out_specs=(pl.BlockSpec(memory_space=VMEM),) * 5,
        compiler_params=params(),
        name="project",
    )(place, ids, cand, *pieces, other)


def score_kernel(lengths, hist, query, self_term, gate, cand, out_weight, rows_ref, out):
    owners, users, per_owner, _ = hist.shape
    width = cand.shape[1]
    head = width // HEADS
    positions = owners * per_owner
    count = cand.shape[0] // users
    lane = iota((1, positions), 1)
    position = (lane % per_owner) * owners + lane // per_owner
    for user in range(users):
        at = slice(user * count, (user + 1) * count)
        length = lengths[user]
        live = position < length
        kv = hist[:, user].reshape(positions, 2 * width)
        parts = []
        for h in range(HEADS):
            cols = slice(h * head, (h + 1) * head)
            scores = lax.dot_general(
                query[at, cols], kv[:, cols], (((1,), (1,)), ((), ())), preferred_element_type=F32
            ) * (head ** (-0.5))
            weights = jnp.where(live, silu(scores), 0.0).astype(BF16)
            parts.append(dot(weights, kv[:, width + h * head : width + (h + 1) * head]))
        attended = (jnp.concatenate(parts, axis=1) + self_term[at]) / (
            length.astype(F32) + 1.0
        )
        center = attended - jnp.mean(attended, axis=-1, keepdims=True)
        spread = jnp.mean(center * center, axis=-1, keepdims=True)
        gated = (center * lax.rsqrt(spread + 1e-06) * gate[at]).astype(BF16)
        final = cand[at].astype(F32) + dot(gated, out_weight[...])
        scale = lax.rsqrt(jnp.mean(final * final, axis=-1, keepdims=True) + 1e-06)
        unit = (final * scale).astype(BF16).astype(F32)
        logit = jnp.sum(unit * rows_ref[at].astype(F32), axis=-1, keepdims=True)
        eye = iota((count, count), 0) == iota((count, count), 1)
        out[user : user + 1, :] = jnp.sum(jnp.where(eye, logit, 0.0), axis=0, keepdims=True)


def score(lengths, hist, query, self_term, gate, cand, out_weight, rows):
    users = hist.shape[1]
    return pl.pallas_call(
        score_kernel,
        out_shape=jax.ShapeDtypeStruct((users, cand.shape[0] // users), F32),
        in_specs=[pl.BlockSpec(memory_space=SMEM)] + [pl.BlockSpec(memory_space=VMEM)] * 7,
        out_specs=pl.BlockSpec(memory_space=VMEM),
        compiler_params=params(),
        name="score",
    )(lengths, hist, query, self_term, gate, cand, out_weight, rows)


def body(
    candidates, proj_weight, out_weight, history_kv, scorer_user, hist_len, cand_item, item_table
):
    users, count, width = candidates.shape
    cand = candidates.reshape(users * count, width)
    x, core = lax.axis_index("x"), lax.axis_index("core")
    item = x * 2 + core
    place = jnp.stack([item, x, core]).astype(jnp.int32)
    owners = lax.axis_size(USER)

    row = spread(place, proj_weight, out_weight, lax.axis_size("z"))
    rows_z = lax.all_to_all(row, "z", split_axis=0, concat_axis=0, tiled=True)

    my_ids = cand_item.reshape(1, users * count)
    ids = lax.all_gather(my_ids, ITEM, axis=0, tiled=True)
    found = fetch(place, ids, item_table)

    hist = history_kv.reshape(history_kv.shape[0], history_kv.shape[1], -1)
    picked = pick(scorer_user, place, hist, ids, owners, users)
    arrived = lax.all_to_all(picked, USER, split_axis=0, concat_axis=0, tiled=True)

    rows_z = block(picked, rows_z, width)
    rows_zy = lax.all_gather(rows_z, "y", axis=0, tiled=True)
    pieces = list(pack_x(found, rows_zy))
    for k in (1, 3, 2):
        pieces[k] = lax.ppermute(pieces[k], "x", [(j, (j + k) % 4) for j in range(4)])
    other = lax.ppermute(pack_core(pieces), "core", [(0, 1), (1, 0)])
    rows, gate, query, self_term, out_w = project(place, my_ids, cand, pieces, other)
    return score(hist_len, arrived, query, self_term, gate, cand, out_w, rows)


def solution(mesh):
    cut = Mesh(mesh.devices.reshape(16, 4, 4, 2), ("z", "y", "x", "core"))
    return jax.shard_map(
        body,
        mesh=cut,
        in_specs=(
            P(USER + ITEM, None, None),
            P(USER, None),
            P(USER, None),
            P(ITEM, None, USER, None),
            P(),
            P(USER + ITEM),
            P(USER + ITEM, None),
            P(ITEM, None),
        ),
        out_specs=P(USER + ITEM, None),
        check_vma=False,
    )
```

time: 241 us -> 107 us (0.44)
  the two profiles are of different devices: /device:TPU:1 before, /device:TPU:8 now
where the time goes in v1:
time: 107 us
  starting transfers between devices  41.8 us (39%)
  waiting for transfers between devices  26 us (24%)
  blocking collectives  23.9 us (22%)
  Pallas kernels  11.4 us (11%)
  local copies, waits for them, and re-layouts  3.38 us (3%)
    ppermute x3, waiting for transfers between devices, body(): lax.ppermute(pieces[k], 'x', [(j, (j + k) % 4) for j in range(4)])  18.8 us
    all_to_all x1, starting transfers between devices, body(): lax.all_to_all(picked, USER, split_axis=0, concat_axis=0, tiled=True)  15.5 us
    all_to_all x1, starting transfers between devices, body(): rows_z = lax.all_to_all(row, 'z', split_axis=0, concat_axis=0, tiled=True)  15.2 us
    all_gather x1, blocking collectives, body(): rows_zy = lax.all_gather(rows_z, 'y', axis=0, tiled=True)  13.1 us
    all_gather x1, blocking collectives, body(): ids = lax.all_gather(my_ids, ITEM, axis=0, tiled=True)  10.8 us
    ppermute x3, starting transfers between devices, body(): lax.ppermute(pieces[k], 'x', [(j, (j + k) % 4) for j in range(4)])  9.18 us
    all_to_all x1, waiting for transfers between devices, body(): lax.all_to_all(picked, USER, split_axis=0, concat_axis=0, tiled=True)  3.63 us
    ppermute x1, waiting for transfers between devices, body(): other = lax.ppermute(pack_core(pieces), 'core', [(0, 1), (1, 0)])  3.56 us
  transfers between devices with their start and end apart: 6, of which 4 were waited for; matrix products, arithmetic and copies ran while one was open for 0% of the time, Pallas kernels for 7%

profile of v1, /device:TPU:8, one launch (start us, length us, event | category | flops | bytes accessed | tf_op | source)
XLA Modules:
  0.0 106.6 jit_solution(3777632778743735491)
XLA Ops:
  0.0 0.1 pad_add_fusion.place
  0.1 0.0 copy-start.3
  0.1 0.8 copy-done.3
  0.8 0.7 copy-done.4
  1.5 1.2 %spread_weight_row.1 = bf16[16,2,1280]{2,1,0:T(2,128)(2,1)} custom-call(s32[3]{0:T(128)S(1)} %pad_add_fusion.place, bf16[8,2048]{1,0:T(8,128)(2,1)S(1)} %copy-done.3, bf16[8,512]{1,0:T(8,128)(2,1)S(1)} %copy-done.4), custom_call_target="tpu_custom_call" | custom-call | tf_op jit(solution)/shard_map/spread_weight_row/pallas_call | solution.py:54
  2.7 15.2 %all-to-all-start.1 = ((bf16[16,2,1280]{2,1,0:T(2,128)(2,1)}), bf16[16,2,1280]{2,1,0:T(2,128)(2,1)S(1)}, u32[]{:S(2)}, u32[]{:S(2)}) async-start(bf16[16,2,1280]{2,1,0:T(2,128)(2,1)} %spread_weight_row.1), calls=%async_computation.1 | async-start | bytes 163840 | tf_op jit(solution)/shard_map/all_to_all | solution.py:323
  18.0 10.8 %all-gather = s32[8,1,256]{2,1,0:T(1,128)S(1)} all-gather(s32[1,1,256]{2,1,0:T(1,128)} %bitcast.15), channel_id=1, replica_groups=mesh['z'=16,'y'=4,'x'=4,'core'=2] {'x','core'}, dimensions={0}, use_global_device_ids=true | all-gather | bytes 9216 | tf_op jit(solution)/shard_map/all_gather | solution.py:326
  28.8 1.2 %copy-done = bf16[128,4,1,1024]{3,1,2,0:T(4,128)(2,1)S(1)} copy-done((bf16[128,4,1,1024]{3,1,2,0:T(4,128)(2,1)S(1)}, bf16[128,4,1,1024]{3,1,2,0:T(4,128)(2,1)}, u32[]{:S(2)}) %copy-start) | copy-done | bytes 1048600
  30.0 0.7 copy-done.5
  30.7 1.9 %pick_history.1.first = bf16[64,2,4,1024]{3,2,1,0:T(4,128)(2,1)} custom-call(s32[1024]{0:T(1024)S(1)} %copy-done.5, s32[3]{0:T(128)S(1)} %pad_add_fusion.place, bf16[128,4,1024]{2,1,0:T(4,128)(2,1)S(1)} %bitcast.10, s32[8,256]{1,0:T(8,128)S(1)} %bitcast.13), custom_call_target="tpu_custom_call" | custom-call | tf_op jit(solution)/shard_map/pick_history/pallas_call | solution.py:99
  32.6 0.0 all-to-all-done.1.rows
  32.6 15.5 %all-to-all-start = ((bf16[64,2,4,1024]{3,2,1,0:T(4,128)(2,1)}), bf16[64,2,4,1024]{3,2,1,0:T(4,128)(2,1)S(1)}, u32[]{:S(2)}, u32[]{:S(2)}) async-start(bf16[64,2,4,1024]{3,2,1,0:T(4,128)(2,1)} %pick_history.1.first), calls=%async_computation | async-start | bytes 2097152 | tf_op jit(solution)/shard_map/all_to_all | solution.py:331
  48.1 0.0 copy-done.1
  48.1 2.3 %fetch_rows.1.found = bf16[4,2,96,512]{3,2,1,0:T(8,128)(2,1)S(1)} custom-call(s32[3]{0:T(128)S(1)} %pad_add_fusion.place, s32[8,256]{1,0:T(8,128)S(1)} %bitcast.14, bf16[1024,512]{1,0:T(8,128)(2,1)S(1)} %copy-done.1), custom_call_target="tpu_custom_call" | custom-call | tf_op jit(solution)/shard_map/fetch_rows/pallas_call | solution.py:140
  50.4 0.2 block_weight_rows.1
  50.6 13.1 %all_gather.7.weight = bf16[320,512]{1,0:T(8,128)(2,1)S(1)} all-gather(bf16[80,512]{1,0:T(8,128)(2,1)S(1)} %block_weight_rows.1), channel_id=1, replica_groups=mesh['z'=16,'y'=4,'x'=4,'core'=2] {'y'}, dimensions={0}, use_global_device_ids=true | all-gather | bytes 409600 | tf_op jit(solution)/shard_map/all_gather | solution.py:334
  63.7 0.1 pack_for_x.1
  63.8 1.9 %collective-permute-start = (bf16[512,512]{1,0:T(8,128)(2,1)S(1)}, bf16[512,512]{1,0:T(8,128)(2,1)S(1)}, u32[]{:S(2)}, u32[]{:S(2)}) collective-permute-start(bf16[512,512]{1,0:T(8,128)(2,1)S(1)} %get-tuple-element.15), channel_id=1, source_target_pairs={{0,2},{2,4},{4,6},{6,0},{1,3},{3,5},{5,7},{7,1},{8,10},{10,12},{12... | collective-permute-start | bytes 1572872 | tf_op jit(solution)/shard_map/ppermute | solution.py:337
  65.7 3.0 %collective-permute-start.1 = (bf16[512,512]{1,0:T(8,128)(2,1)S(1)}, bf16[512,512]{1,0:T(8,128)(2,1)S(1)}, u32[]{:S(2)}, u32[]{:S(2)}) collective-permute-start(bf16[512,512]{1,0:T(8,128)(2,1)S(1)} %get-tuple-element.16), channel_id=1, source_target_pairs={{0,4},{2,6},{4,0},{6,2},{1,5},{3,7},{5,1},{7,3},{8,12},{10,14},{12... | collective-permute-start | bytes 1572872 | tf_op jit(solution)/shard_map/ppermute | solution.py:337
  68.7 4.3 %collective-permute-start.2 = (bf16[512,512]{1,0:T(8,128)(2,1)S(1)}, bf16[512,512]{1,0:T(8,128)(2,1)S(1)}, u32[]{:S(2)}, u32[]{:S(2)}) collective-permute-start(bf16[512,512]{1,0:T(8,128)(2,1)S(1)} %get-tuple-element.17), channel_id=1, source_target_pairs={{0,6},{2,0},{4,2},{6,4},{1,7},{3,1},{5,3},{7,5},{8,14},{10,8},{12,... | collective-permute-start | bytes 1572872 | tf_op jit(solution)/shard_map/ppermute | solution.py:337
  73.0 16.2 %collective-permute-done.refs_1_.p1 = bf16[512,512]{1,0:T(8,128)(2,1)S(1)} collective-permute-done((bf16[512,512]{1,0:T(8,128)(2,1)S(1)}, bf16[512,512]{1,0:T(8,128)(2,1)S(1)}, u32[]{:S(2)}, u32[]{:S(2)}) %collective-permute-start) | collective-permute-done | bytes 524320 | tf_op jit(solution)/shard_map/ppermute | solution.py:337
  89.2 0.0 collective-permute-done.1.refs_2_.p2
  89.2 2.5 %collective-permute-done.2.refs_3_.p3 = bf16[512,512]{1,0:T(8,128)(2,1)S(1)} collective-permute-done((bf16[512,512]{1,0:T(8,128)(2,1)S(1)}, bf16[512,512]{1,0:T(8,128)(2,1)S(1)}, u32[]{:S(2)}, u32[]{:S(2)}) %collective-permute-start.2) | collective-permute-done | bytes 524320 | tf_op jit(solution)/shard_map/ppermute | solution.py:337
  91.8 0.1 pack_for_core.1
  91.9 1.9 %collective-permute-start.3 = (bf16[4,416,512]{2,1,0:T(8,128)(2,1)S(1)}, bf16[4,416,512]{2,1,0:T(8,128)(2,1)S(1)}, u32[]{:S(2)}, u32[]{:S(2)}) collective-permute-start(bf16[4,416,512]{2,1,0:T(8,128)(2,1)S(1)} %pack_for_core.1), channel_id=1, source_target_pairs={{0,1},{1,0},{2,3},{3,2},{4,5},{5,4},{6,7},{7,6},{8,9},{9,8},{10,11... | collective-permute-start | bytes 5111816 | tf_op jit(solution)/shard_map/ppermute | solution.py:338
  93.8 3.6 %collective-permute-done.3.other = bf16[4,416,512]{2,1,0:T(8,128)(2,1)S(1)} collective-permute-done((bf16[4,416,512]{2,1,0:T(8,128)(2,1)S(1)}, bf16[4,416,512]{2,1,0:T(8,128)(2,1)S(1)}, u32[]{:S(2)}, u32[]{:S(2)}) %collective-permute-start.3) | collective-permute-done | bytes 1703968 | tf_op jit(solution)/shard_map/ppermute | solution.py:338
  97.4 0.0 copy-done.2
  97.4 0.0 copy-done.6
  97.4 2.7 %project.1 = (bf16[256,512]{1,0:T(8,128)(2,1)S(1)}, f32[256,512]{1,0:T(8,128)S(1)}, bf16[256,512]{1,0:T(8,128)(2,1)S(1)}, f32[256,512]{1,0:T(8,128)S(1)}, bf16[512,512]{1,0:T(8,128)(2,1)S(1)}) custom-call(s32[3]{0:T(128)S(1)} %pad_add_fusion.place, s32[1,256]{1,0:T(1,128)S(1)} %bitcast.16, bf16[256,512]{1,0:T(8,128)(2,1)S(1)} %bitcast.11, ...), custom_call_target="tpu_custom_call" | custom-call | tf_op jit(solution)/shard_map/project/pallas_call | solution.py:249
  100.1 3.6 %all-to-all-done.hist = bf16[64,2,4,1024]{3,2,1,0:T(4,128)(2,1)S(1)} async-done(((bf16[64,2,4,1024]{3,2,1,0:T(4,128)(2,1)}), bf16[64,2,4,1024]{3,2,1,0:T(4,128)(2,1)S(1)}, u32[]{:S(2)}, u32[]{:S(2)}) %all-to-all-start) | async-done | bytes 1048608 | tf_op jit(solution)/shard_map/all_to_all | solution.py:331
  103.8 0.0 copy-done.7
  103.8 2.8 %score.1 = f32[2,128]{1,0:T(2,128)} custom-call(s32[2]{0:T(128)S(1)} %copy-done.7, bf16[64,2,4,1024]{3,2,1,0:T(4,128)(2,1)S(1)} %all-to-all-done.hist, bf16[256,512]{1,0:T(8,128)(2,1)S(1)} %get-tuple-element.18.query, f32[256,512]{1,0:T(8,128)S(1)} %get-tuple-element.19.self_term, f32[256,512]{1,0:T(8,128)S(1)} %get-tuple-element.20.gate, ...), custom_call_target="tpu_custom_call" | custom-call | tf_op jit(solution)/shard_map/score/pallas_call | solution.py:302
  (8 shorter events, 0.0 us)
Async XLA Ops:
  0.1 0.8 copy-start.3
  0.8 0.7 copy-start.4
  2.7 29.8 %all-to-all-start.1 = ((bf16[16,2,1280]{2,1,0:T(2,128)(2,1)}), bf16[16,2,1280]{2,1,0:T(2,128)(2,1)S(1)}, u32[]{:S(2)}, u32[]{:S(2)}) async-start(bf16[16,2,1280]{2,1,0:T(2,128)(2,1)} %spread_weight_row.1), calls=%async_computation.1 | async-start | bytes 163840 | tf_op jit(solution)/shard_map/all_to_all | solution.py:323
  28.8 1.2 %copy-start = (bf16[128,4,1,1024]{3,1,2,0:T(4,128)(2,1)S(1)}, bf16[128,4,1,1024]{3,1,2,0:T(4,128)(2,1)}, u32[]{:S(2)}) copy-start(bf16[128,4,1,1024]{3,1,2,0:T(4,128)(2,1)} %param.11) | copy-start | bytes 3145732
  30.0 0.7 copy-start.5
  30.7 17.5 %copy-start.1 = (bf16[1024,512]{1,0:T(8,128)(2,1)S(1)}, bf16[1024,512]{1,0:T(8,128)(2,1)}, u32[]{:S(2)}) copy-start(bf16[1024,512]{1,0:T(8,128)(2,1)} %table.1) | copy-start | bytes 3145732
  32.6 71.2 %all-to-all-start = ((bf16[64,2,4,1024]{3,2,1,0:T(4,128)(2,1)}), bf16[64,2,4,1024]{3,2,1,0:T(4,128)(2,1)S(1)}, u32[]{:S(2)}, u32[]{:S(2)}) async-start(bf16[64,2,4,1024]{3,2,1,0:T(4,128)(2,1)} %pick_history.1.first), calls=%async_computation | async-start | bytes 2097152 | tf_op jit(solution)/shard_map/all_to_all | solution.py:331
  63.8 25.4 %collective-permute-start = (bf16[512,512]{1,0:T(8,128)(2,1)S(1)}, bf16[512,512]{1,0:T(8,128)(2,1)S(1)}, u32[]{:S(2)}, u32[]{:S(2)}) collective-permute-start(bf16[512,512]{1,0:T(8,128)(2,1)S(1)} %get-tuple-element.15), channel_id=1, source_target_pairs={{0,2},{2,4},{4,6},{6,0},{1,3},{3,5},{5,7},{7,1},{8,10},{10,12},{12... | collective-permute-start | bytes 1572872 | tf_op jit(solution)/shard_map/ppermute | solution.py:337
  65.7 23.5 %collective-permute-start.1 = (bf16[512,512]{1,0:T(8,128)(2,1)S(1)}, bf16[512,512]{1,0:T(8,128)(2,1)S(1)}, u32[]{:S(2)}, u32[]{:S(2)}) collective-permute-start(bf16[512,512]{1,0:T(8,128)(2,1)S(1)} %get-tuple-element.16), channel_id=1, source_target_pairs={{0,4},{2,6},{4,0},{6,2},{1,5},{3,7},{5,1},{7,3},{8,12},{10,14},{12... | collective-permute-start | bytes 1572872 | tf_op jit(solution)/shard_map/ppermute | solution.py:337
  68.7 23.1 %collective-permute-start.2 = (bf16[512,512]{1,0:T(8,128)(2,1)S(1)}, bf16[512,512]{1,0:T(8,128)(2,1)S(1)}, u32[]{:S(2)}, u32[]{:S(2)}) collective-permute-start(bf16[512,512]{1,0:T(8,128)(2,1)S(1)} %get-tuple-element.17), channel_id=1, source_target_pairs={{0,6},{2,0},{4,2},{6,4},{1,7},{3,1},{5,3},{7,5},{8,14},{10,8},{12,... | collective-permute-start | bytes 1572872 | tf_op jit(solution)/shard_map/ppermute | solution.py:337
  91.8 5.6 %copy-start.2 = (bf16[2,128,512]{2,1,0:T(8,128)(2,1)S(1)}, bf16[2,128,512]{2,1,0:T(8,128)(2,1)}, u32[]{:S(2)}) copy-start(bf16[2,128,512]{2,1,0:T(8,128)(2,1)} %param.8) | copy-start | bytes 786436
  91.8 5.6 %copy-start.6 = (s32[2,128]{1,0:T(2,128)S(1)}, s32[2,128]{1,0:T(2,128)}, u32[]{:S(2)}) copy-start(s32[2,128]{1,0:T(2,128)} %param.14) | copy-start | bytes 3076
  91.9 5.5 %collective-permute-start.3 = (bf16[4,416,512]{2,1,0:T(8,128)(2,1)S(1)}, bf16[4,416,512]{2,1,0:T(8,128)(2,1)S(1)}, u32[]{:S(2)}, u32[]{:S(2)}) collective-permute-start(bf16[4,416,512]{2,1,0:T(8,128)(2,1)S(1)} %pack_for_core.1), channel_id=1, source_target_pairs={{0,1},{1,0},{2,3},{3,2},{4,5},{5,4},{6,7},{7,6},{8,9},{9,8},{10,11... | collective-permute-start | bytes 5111816 | tf_op jit(solution)/shard_map/ppermute | solution.py:338
  97.4 6.4 %copy-start.7 = (s32[2]{0:T(128)S(1)}, s32[2]{0:T(128)}, u32[]{:S(2)}) copy-start(s32[2]{0:T(128)} %lengths.1) | copy-start | bytes 28

commit v2 on v1

v2 whole, which is shorter than its diff:
```python
import functools

import jax
import jax.numpy as jnp
from jax import lax
from jax.experimental import pallas as pl
from jax.experimental.pallas import tpu as pltpu
from jax.sharding import Mesh, PartitionSpec as P

HEADS = 4
CAP = 96
F32 = jnp.float32
BF16 = jnp.bfloat16
VMEM = pltpu.VMEM
SMEM = pltpu.SMEM
VMEM_LIMIT = 40 * 1024 * 1024

USER = ("z", "y")
ITEM = ("x", "core")


def params():
    return pltpu.CompilerParams(vmem_limit_bytes=VMEM_LIMIT)


def silu(values):
    return values * jax.nn.sigmoid(values)


def iota(shape, dim):
    return lax.broadcasted_iota(jnp.int32, shape, dim)


def dot(a, b):
    return jnp.dot(a, b, preferred_element_type=F32)


def shard_kernel(proj_weight, out_weight, out):
    width = out.shape[1]
    wide = proj_weight[...].astype(F32)
    parts = [wide[:, k * width : (k + 1) * width] for k in range(4)]
    parts.append(out_weight[...].astype(F32))
    out[...] = jnp.concatenate(parts, axis=0).astype(BF16)


def stack_shard(proj_weight, out_weight):
    rows, width = out_weight.shape
    return pl.pallas_call(
        shard_kernel,
        out_shape=jax.ShapeDtypeStruct((rows * 5, width), BF16),
        in_specs=[pl.BlockSpec(memory_space=VMEM)] * 2,
        out_specs=pl.BlockSpec(memory_space=VMEM),
        compiler_params=params(),
        name="stack_weight_shard",
    )(proj_weight, out_weight)


def block_kernel(p0, p1, my_ids, other_ids, out):
    rows = jnp.concatenate([p0[...].astype(F32), p1[...].astype(F32)], axis=0).astype(BF16)
    count = rows.shape[0]
    k = iota((count, count), 0)
    source = (k % 16) // 8 * (count // 2) + k // 16 * 8 + k % 8
    move = (iota((count, count), 1) == source).astype(BF16)
    ids = jnp.concatenate([my_ids[...], other_ids[...]], axis=0)
    digits = jnp.concatenate([ids // 128, ids % 128], axis=1).astype(F32)
    rest = jnp.zeros((out.shape[0] - count - 2, out.shape[1]), F32)
    out[...] = jnp.concatenate([dot(move, rows), digits, rest], axis=0).astype(BF16)


def block(p0, p1, my_ids, other_ids):
    rows, width = p0.shape
    return pl.pallas_call(
        block_kernel,
        out_shape=jax.ShapeDtypeStruct((2 * rows + 16, width), BF16),
        in_specs=[pl.BlockSpec(memory_space=VMEM)] * 4,
        out_specs=pl.BlockSpec(memory_space=VMEM),
        compiler_params=params(),
        name="block_weights_and_ids",
    )(p0, p1, my_ids, other_ids)


def pick_kernel(slots, place, hist, out):
    item = place[0]
    owners = out.shape[0]
    users = out.shape[1]
    group = hist.shape[0]

    def one(owner, carry):
        for slot in range(users):
            local = slots[(owner * 8 + item) * users + slot] - item * group
            out[owner, slot] = hist[local]
        return carry

    lax.fori_loop(0, owners, one, 0, unroll=4)


def pick(scorer_user, place, hist, owners, users):
    return pl.pallas_call(
        pick_kernel,
        out_shape=jax.ShapeDtypeStruct((owners, users) + hist.shape[1:], hist.dtype),
        in_specs=[
            pl.BlockSpec(memory_space=SMEM),
            pl.BlockSpec(memory_space=SMEM),
            pl.BlockSpec(memory_space=VMEM),
        ],
        out_specs=pl.BlockSpec(memory_space=VMEM),
        compiler_params=params(),
        name="pick_history",
    )(scorer_user, place, hist)


def fetch_kernel(place, gathered, table, *outs):
    item, x = place[0], place[1]
    rows = table.shape[0]
    step = gathered.shape[0] // 4
    parts = []
    for k in range(4):
        at = pl.multiple_of((x + k) % 4 * step + step - 16, 16)
        parts.append(gathered[pl.ds(at, 16), :].astype(F32)[:2])
    digits = jnp.concatenate(parts, axis=0)
    count = digits.shape[1] // 2
    local = digits[:, :count] * 128.0 + digits[:, count:] - (item * rows).astype(F32)
    mine = (local >= 0.0) & (local < float(rows))
    before = (iota((count, count), 0) < iota((count, count), 1)).astype(BF16)
    rank = dot(mine.astype(F32).astype(BF16), before)
    key = jnp.where(mine, rank, -1.0)
    tab = table[...]
    slot = iota((CAP, count), 0).astype(F32)
    for k in range(8):
        match = slot == key[k : k + 1]
        row_of = jnp.sum(jnp.where(match, local[k : k + 1], 0.0), axis=1, keepdims=True)
        hot = (iota((CAP, rows), 1).astype(F32) == row_of).astype(BF16)
        at = (k % 2) * CAP
        outs[k // 2][at : at + CAP] = dot(hot, tab).astype(BF16)


def fetch(place, gathered, table):
    return pl.pallas_call(
        fetch_kernel,
        out_shape=(jax.ShapeDtypeStruct((2 * CAP, table.shape[1]), table.dtype),) * 4,
        in_specs=[pl.BlockSpec(memory_space=SMEM)] + [pl.BlockSpec(memory_space=VMEM)] * 2,
        out_specs=(pl.BlockSpec(memory_space=VMEM),) * 4,
        compiler_params=params(),
        name="fetch_rows",
    )(place, gathered, table)


def strip_kernel(gathered, out):
    step, keep = gathered.shape[0] // 4, out.shape[0] // 4
    for k in range(4):
        out[k * keep : (k + 1) * keep] = gathered[k * step : k * step + keep]


def strip(gathered):
    rows, width = gathered.shape
    return pl.pallas_call(
        strip_kernel,
        out_shape=jax.ShapeDtypeStruct((rows - 64, width), BF16),
        in_specs=[pl.BlockSpec(memory_space=VMEM)],
        out_specs=pl.BlockSpec(memory_space=VMEM),
        compiler_params=params(),
        name="strip_ids",
    )(gathered)


def pack_kernel(starts, *refs):
    out = refs[-1]
    at = 0
    for start, ref in zip(starts, refs[:-1]):
        rows = ref.shape[0] - start
        out[at : at + rows] = ref[start:]
        at += rows


def pack(starts, pieces):
    rows = sum(piece.shape[0] - start for start, piece in zip(starts, pieces))
    return pl.pallas_call(
        functools.partial(pack_kernel, starts),
        out_shape=jax.ShapeDtypeStruct((rows, pieces[0].shape[1]), BF16),
        in_specs=[pl.BlockSpec(memory_space=VMEM)] * len(pieces),
        out_specs=pl.BlockSpec(memory_space=VMEM),
        compiler_params=params(),
        name="pack_for_core",
    )(*pieces)


def proj_kernel(
    place, cand, w0, w1, w2a, w2b, w3, other, gate, query, self_term, out_weight
):
    core = place[2]
    rows, width = cand.shape
    values = cand[...].astype(F32)
    center = values - jnp.mean(values, axis=-1, keepdims=True)
    spread = jnp.mean(center * center, axis=-1, keepdims=True)
    normed = (center * lax.rsqrt(spread + 1e-06)).astype(BF16)
    g = iota((width, width), 1)
    peer = (g // 16) % 4 * 2 + (core + g // 256) % 2
    from_z = (place[4] + 32 - peer - (g // 8) % 2 * 8) % 16
    from_y = (place[3] + 4 - (g // 64) % 4) % 4
    natural = from_z * 32 + from_y * 8 + g % 8
    perm = (iota((width, width), 0) == natural).astype(BF16)
    normed = dot(normed, perm).astype(BF16)
    shard = w0.shape[0]

    def weight(cols):
        parts = [(k * 5 + cols) * 16 for k in range(4)]
        own = [(ref, at) for ref in (w0, w1) for at in parts]
        own += [(w2a, parts[0]), (w2a, parts[1])]
        own += [(w2b, parts[2] - shard // 2), (w2b, parts[3] - shard // 2)]
        own += [(w3, at) for at in parts]
        own += [(other, k * shard + at) for k in range(4) for at in parts]
        return jnp.concatenate([ref[at : at + 16] for ref, at in own], axis=0)

    out_weight[...] = dot(perm, weight(4)).astype(BF16)
    gate[...] = silu(dot(normed, weight(0)))
    value = silu(dot(normed, weight(1))).astype(BF16).astype(F32)
    q = silu(dot(normed, weight(2))).astype(BF16)
    k = silu(dot(normed, weight(3))).astype(BF16)
    query[...] = q
    product = q.astype(F32) * k.astype(F32)
    head = width // HEADS
    for h in range(HEADS):
        cols = slice(h * head, (h + 1) * head)
        score = jnp.sum(product[:, cols], axis=-1, keepdims=True) * head ** (-0.5)
        self_term[:, cols] = silu(score).astype(BF16).astype(F32) * value[:, cols]


def project(place, cand, pieces, other):
    rows, width = cand.shape
    return pl.pallas_call(
        proj_kernel,
        out_shape=(
            jax.ShapeDtypeStruct((rows, width), F32),
            jax.ShapeDtypeStruct((rows, width), BF16),
            jax.ShapeDtypeStruct((rows, width), F32),
            jax.ShapeDtypeStruct((width, width), BF16),
        ),
        in_specs=[pl.BlockSpec(memory_space=SMEM)] + [pl.BlockSpec(memory_space=VMEM)] * 7,
        out_specs=(pl.BlockSpec(memory_space=VMEM),) * 4,
        compiler_params=params(),
        name="project",
        cost_estimate=pl.CostEstimate(flops=int(2e10), bytes_accessed=0, transcendentals=0),
    )(place, cand, *pieces, other)


def order_kernel(place, ids, f0, f1, f2, f3, other, out):
    own = (f0, f1, f2, f3)
    x, core = place[1], place[2]
    rows, width = out.shape
    shard = ids[...] // 1024
    before = (iota((rows, rows), 0) < iota((rows, rows), 1)).astype(BF16)
    hot = iota((8, rows), 0) == shard
    ranks = dot(hot.astype(BF16), before)
    rank = jnp.sum(jnp.where(hot, ranks, 0.0), axis=0, keepdims=True)
    offset = ((x + 4 - shard // 2) % 4) * 2 + (core + 2 - shard % 2) % 2
    total = jnp.zeros((rows, width), F32)
    for j in range(8):
        key = jnp.where(offset == j, rank, -1.0)
        chosen = (iota((CAP, rows), 0).astype(F32) == key).astype(BF16)
        at = other.shape[0] - (4 - j // 2) * CAP
        piece = other[at : at + CAP] if j % 2 else own[j // 2][:CAP]
        total += lax.dot_general(
            chosen, piece, (((0,), (0,)), ((), ())), preferred_element_type=F32
        )
    out[...] = total.astype(BF16)


def order(place, ids, pieces, other):
    return pl.pallas_call(
        order_kernel,
        out_shape=jax.ShapeDtypeStruct((ids.shape[1], other.shape[1]), BF16),
        in_specs=[pl.BlockSpec(memory_space=SMEM)] + [pl.BlockSpec(memory_space=VMEM)] * 6,
        out_specs=pl.BlockSpec(memory_space=VMEM),
        compiler_params=params(),
        name="order_rows",
    )(place, ids, *pieces, other)


def score_kernel(lengths, hist, query, self_term, gate, cand, out_weight, rows_ref, out):
    owners, users, per_owner, _ = hist.shape
    width = cand.shape[1]
    head = width // HEADS
    positions = owners * per_owner
    count = cand.shape[0] // users
    lane = iota((1, positions), 1)
    position = (lane % per_owner) * owners + lane // per_owner
    for user in range(users):
        at = slice(user * count, (user + 1) * count)
        length = lengths[user]
        live = position < length
        kv = hist[:, user].reshape(positions, 2 * width)
        parts = []
        for h in range(HEADS):
            cols = slice(h * head, (h + 1) * head)
            scores = lax.dot_general(
                query[at, cols], kv[:, cols], (((1,), (1,)), ((), ())), preferred_element_type=F32
            ) * (head ** (-0.5))
            weights = jnp.where(live, silu(scores), 0.0).astype(BF16)
            parts.append(dot(weights, kv[:, width + h * head : width + (h + 1) * head]))
        attended = (jnp.concatenate(parts, axis=1) + self_term[at]) / (
            length.astype(F32) + 1.0
        )
        center = attended - jnp.mean(attended, axis=-1, keepdims=True)
        spread = jnp.mean(center * center, axis=-1, keepdims=True)
        gated = (center * lax.rsqrt(spread + 1e-06) * gate[at]).astype(BF16)
        final = cand[at].astype(F32) + dot(gated, out_weight[...])
        scale = lax.rsqrt(jnp.mean(final * final, axis=-1, keepdims=True) + 1e-06)
        unit = (final * scale).astype(BF16).astype(F32)
        logit = jnp.sum(unit * rows_ref[at].astype(F32), axis=-1, keepdims=True)
        eye = iota((count, count), 0) == iota((count, count), 1)
        out[user : user + 1, :] = jnp.sum(jnp.where(eye, logit, 0.0), axis=0, keepdims=True)


def score(lengths, hist, query, self_term, gate, cand, out_weight, rows):
    users = hist.shape[1]
    return pl.pallas_call(
        score_kernel,
        out_shape=jax.ShapeDtypeStruct((users, cand.shape[0] // users), F32),
        in_specs=[pl.BlockSpec(memory_space=SMEM)] + [pl.BlockSpec(memory_space=VMEM)] * 7,
        out_specs=pl.BlockSpec(memory_space=VMEM),
        compiler_params=params(),
        name="score",
    )(lengths, hist, query, self_term, gate, cand, out_weight, rows)


def along(axis, values, offset):
    size = lax.axis_size(axis)
    return lax.ppermute(values, axis, [(j, (j + offset) % size) for j in range(size)])


def swap_core(values):
    return lax.ppermute(values, "core", [(0, 1), (1, 0)])


def body(
    candidates, proj_weight, out_weight, history_kv, scorer_user, hist_len, cand_item, item_table
):
    users, count, width = candidates.shape
    cand = candidates.reshape(users * count, width)
    x, core = lax.axis_index("x"), lax.axis_index("core")
    item = x * 2 + core
    y, z = lax.axis_index("y"), lax.axis_index("z")
    place = jnp.stack([item, x, core, y, z]).astype(jnp.int32)
    owners = lax.axis_size(USER)

    shard = stack_shard(proj_weight, out_weight)
    zs, items = lax.axis_size("z"), lax.axis_size(ITEM)
    shards = [
        lax.ppermute(
            shard,
            ("z",) + ITEM,
            [
                (k * items + i, (k + i + step) % zs * items + i)
                for k in range(zs)
                for i in range(items)
            ],
        )
        for step in (8, 0)
    ][::-1]
    my_ids = cand_item.reshape(1, users * count)
    other_ids = swap_core(my_ids)

    hist = history_kv.reshape(history_kv.shape[0], history_kv.shape[1], -1)
    picked = pick(scorer_user, place, hist, owners, users)
    arrived = lax.all_to_all(picked, USER, split_axis=0, concat_axis=0, tiled=True)

    gathered = lax.all_gather(block(*shards, my_ids, other_ids), "x", axis=0, tiled=True)
    weight = strip(gathered)
    half = weight.shape[0] // 2
    left, right = along("y", weight, 1), along("y", weight, 3)
    far_top, far_end = along("y", left[:half], 1), along("y", right[half:], 3)
    pieces = [weight, left, far_top, far_end, right]

    found = list(fetch(place, gathered, item_table))
    for k in (1, 3, 2):
        found[k] = along("x", found[k], k)
    other = swap_core(pack((0,) * 5 + (CAP,) * 4, pieces + found))
    gate, query, self_term, out_w = project(place, cand, pieces, other)
    rows = order(place, my_ids, found, other)
    return score(hist_len, arrived, query, self_term, gate, cand, out_w, rows)


def solution(mesh):
    cut = Mesh(mesh.devices.reshape(16, 4, 4, 2), ("z", "y", "x", "core"))
    return jax.shard_map(
        body,
        mesh=cut,
        in_specs=(
            P(USER + ITEM, None, None),
            P(USER, None),
            P(USER, None),
            P(ITEM, None, USER, None),
            P(),
            P(USER + ITEM),
            P(USER + ITEM, None),
            P(ITEM, None),
        ),
        out_specs=P(USER + ITEM, None),
        check_vma=False,
    )
```

time: 107 us -> 95.4 us (0.89)
  the two profiles are of different devices: /device:TPU:8 before, /device:TPU:6 now
where the time goes in v2:
time: 95.4 us; the launch traced here: 94.7 us
  starting transfers between devices  55.3 us (58%)
  blocking collectives  12.5 us (13%)
  waiting for transfers between devices  12.3 us (13%)
  Pallas kernels  10.9 us (11%)
  local copies, waits for them, and re-layouts  3.5 us (4%)
    ppermute x7, starting transfers between devices, along(): lax.ppermute(values, axis, [(j, (j + offset) % size) for j in range(size)])  22.7 us
    ppermute x2, starting transfers between devices, body(): lax.ppermute(shard, ('z',) + ITEM, [(k * items + i, (k + i + step) % zs *...  14.6 us
    all_to_all x1, starting transfers between devices, body(): lax.all_to_all(picked, USER, split_axis=0, concat_axis=0, tiled=True)  13 us
    all_gather x1, blocking collectives, body(): lax.all_gather(block(*shards, my_ids, other_ids), 'x', axis=0, tiled=True)  12.5 us
    all_to_all x1, waiting for transfers between devices, body(): lax.all_to_all(picked, USER, split_axis=0, concat_axis=0, tiled=True)  5.61 us
    ppermute x2, starting transfers between devices, swap_core(): return lax.ppermute(values, 'core', [(0, 1), (1, 0)])  5.05 us
    ppermute x2, waiting for transfers between devices, swap_core(): return lax.ppermute(values, 'core', [(0, 1), (1, 0)])  3.57 us
    unnamed x16, local copies, waits for them, and re-layouts  3.39 us
  transfers between devices with their start and end apart: 12, of which 4 were waited for; matrix products, arithmetic and copies ran while one was open for 0% of the time, Pallas kernels for 8%

profile of v2, /device:TPU:6, one launch (start us, length us, event | category | flops | bytes accessed | tf_op | source)
XLA Modules:
  0.0 94.7 jit_solution(10308957369356613798)
XLA Ops:
  0.0 0.8 copy-done.3
  0.8 0.7 copy-done.4
  1.5 11.8 %collective-permute-start = (bf16[40,512]{1,0:T(8,128)(2,1)S(1)}, bf16[40,512]{1,0:T(8,128)(2,1)S(1)}, u32[]{:S(2)}, u32[]{:S(2)}) collective-permute-start(bf16[40,512]{1,0:T(8,128)(2,1)S(1)} %stack_weight_shard.1), channel_id=1, source_target_pairs={{0,0},{1,33},{2,66},{3,99},{4,132},{5,165},{6,198},{7,231},{32,32}... | collective-permute-start | bytes 122888 | tf_op jit(solution)/shard_map/ppermute | solution.py:349
  13.3 2.8 %collective-permute-start.1 = (bf16[40,512]{1,0:T(8,128)(2,1)S(1)}, bf16[40,512]{1,0:T(8,128)(2,1)S(1)}, u32[]{:S(2)}, u32[]{:S(2)}) collective-permute-start(bf16[40,512]{1,0:T(8,128)(2,1)S(1)} %stack_weight_shard.1), channel_id=1, source_target_pairs={{0,256},{1,289},{2,322},{3,355},{4,388},{5,421},{6,454},{7,487},{3... | collective-permute-start | bytes 122888 | tf_op jit(solution)/shard_map/ppermute | solution.py:349
  16.0 3.0 %collective-permute-start.2 = (s32[1,256]{1,0:T(1,128)}, s32[1,256]{1,0:T(1,128)S(1)}, u32[]{:S(2)}, u32[]{:S(2)}) collective-permute-start(s32[1,256]{1,0:T(1,128)} %bitcast.11), channel_id=1, source_target_pairs={{0,1},{1,0},{2,3},{3,2},{4,5},{5,4},{6,7},{7,6},{8,9},{9,8},{10,11... | collective-permute-start | bytes 3080 | tf_op jit(solution)/shard_map/ppermute | solution.py:332
  19.1 0.1 stack.23.place
  19.1 1.2 %copy-done = bf16[128,4,1,1024]{3,1,2,0:T(4,128)(2,1)S(1)} copy-done((bf16[128,4,1,1024]{3,1,2,0:T(4,128)(2,1)S(1)}, bf16[128,4,1,1024]{3,1,2,0:T(4,128)(2,1)}, u32[]{:S(2)}) %copy-start) | copy-done | bytes 1048600
  20.4 0.7 copy-done.5
  21.1 1.9 %pick_history.1 = bf16[64,2,4,1024]{3,2,1,0:T(4,128)(2,1)} custom-call(s32[1024]{0:T(1024)S(1)} %copy-done.5, s32[5]{0:T(128)S(1)} %stack.23.place, bf16[128,4,1024]{2,1,0:T(4,128)(2,1)S(1)} %bitcast.8), custom_call_target="tpu_custom_call" | custom-call | tf_op jit(solution)/shard_map/pick_history/pallas_call | solution.py:98
  23.0 13.0 %all-to-all-start = ((bf16[64,2,4,1024]{3,2,1,0:T(4,128)(2,1)}), bf16[64,2,4,1024]{3,2,1,0:T(4,128)(2,1)S(1)}, u32[]{:S(2)}, u32[]{:S(2)}) async-start(bf16[64,2,4,1024]{3,2,1,0:T(4,128)(2,1)} %pick_history.1), calls=%async_computation | async-start | bytes 2097152 | tf_op jit(solution)/shard_map/all_to_all | solution.py:365
  36.0 0.0 collective-permute-done.2.other_ids
  36.0 0.1 block_weights_and_ids.1
  36.2 12.5 %all_gather.3.gathered = bf16[384,512]{1,0:T(8,128)(2,1)S(1)} all-gather(bf16[96,512]{1,0:T(8,128)(2,1)S(1)} %block_weights_and_ids.1), channel_id=1, replica_groups=mesh['z'=16,'y'=4,'x'=4,'core'=2] {'x'}, dimensions={0}, use_global_device_ids=true | all-gather | bytes 491520 | tf_op jit(solution)/shard_map/all_gather | solution.py:367
  48.7 3.7 %collective-permute-start.3 = (bf16[320,512]{1,0:T(8,128)(2,1)S(1)}, bf16[320,512]{1,0:T(8,128)(2,1)S(1)}, u32[]{:S(2)}, u32[]{:S(2)}) collective-permute-start(bf16[320,512]{1,0:T(8,128)(2,1)S(1)} %strip_ids.1.refs_0_.w0), channel_id=1, source_target_pairs={{0,8},{8,16},{16,24},{24,0},{1,9},{9,17},{17,25},{25,1},{2,10},{10... | collective-permute-start | bytes 983048 | tf_op jit(solution)/shard_map/ppermute | solution.py:328
  52.4 3.3 %collective-permute-start.5 = (bf16[320,512]{1,0:T(8,128)(2,1)S(1)}, bf16[320,512]{1,0:T(8,128)(2,1)S(1)}, u32[]{:S(2)}, u32[]{:S(2)}) collective-permute-start(bf16[320,512]{1,0:T(8,128)(2,1)S(1)} %strip_ids.1.refs_0_.w0), channel_id=1, source_target_pairs={{0,24},{8,0},{16,8},{24,16},{1,25},{9,1},{17,9},{25,17},{2,26},{10... | collective-permute-start | bytes 983048 | tf_op jit(solution)/shard_map/ppermute | solution.py:328
  55.8 2.3 %fetch_rows.1 = (bf16[192,512]{1,0:T(8,128)(2,1)S(1)}, bf16[192,512]{1,0:T(8,128)(2,1)S(1)}, bf16[192,512]{1,0:T(8,128)(2,1)S(1)}, bf16[192,512]{1,0:T(8,128)(2,1)S(1)}) custom-call(s32[5]{0:T(128)S(1)} %stack.23.place, bf16[384,512]{1,0:T(8,128)(2,1)S(1)} %all_gather.3.gathered, bf16[1024,512]{1,0:T(8,128)(2,1)S(1)} %copy-done.1), custom_call_target="tpu_custom_call" | custom-call | tf_op jit(solution)/shard_map/fetch_rows/pallas_call | solution.py:138
  58.0 2.7 %collective-permute-start.7 = (bf16[192,512]{1,0:T(8,128)(2,1)S(1)}, bf16[192,512]{1,0:T(8,128)(2,1)S(1)}, u32[]{:S(2)}, u32[]{:S(2)}) collective-permute-start(bf16[192,512]{1,0:T(8,128)(2,1)S(1)} %get-tuple-element.14), channel_id=1, source_target_pairs={{0,2},{2,4},{4,6},{6,0},{1,3},{3,5},{5,7},{7,1},{8,10},{10,12},{12... | collective-permute-start | bytes 589832 | tf_op jit(solution)/shard_map/ppermute | solution.py:328
  60.8 2.8 %collective-permute-start.8 = (bf16[192,512]{1,0:T(8,128)(2,1)S(1)}, bf16[192,512]{1,0:T(8,128)(2,1)S(1)}, u32[]{:S(2)}, u32[]{:S(2)}) collective-permute-start(bf16[192,512]{1,0:T(8,128)(2,1)S(1)} %get-tuple-element.15), channel_id=1, source_target_pairs={{0,4},{2,6},{4,0},{6,2},{1,5},{3,7},{5,1},{7,3},{8,12},{10,14},{12... | collective-permute-start | bytes 589832 | tf_op jit(solution)/shard_map/ppermute | solution.py:328
  63.5 3.1 %collective-permute-start.9 = (bf16[192,512]{1,0:T(8,128)(2,1)S(1)}, bf16[192,512]{1,0:T(8,128)(2,1)S(1)}, u32[]{:S(2)}, u32[]{:S(2)}) collective-permute-start(bf16[192,512]{1,0:T(8,128)(2,1)S(1)} %get-tuple-element.16), channel_id=1, source_target_pairs={{0,6},{2,0},{4,2},{6,4},{1,7},{3,1},{5,3},{7,5},{8,14},{10,8},{12,... | collective-permute-start | bytes 589832 | tf_op jit(solution)/shard_map/ppermute | solution.py:328
  66.7 2.5 %collective-permute-start.4 = (bf16[160,512]{1,0:T(8,128)(2,1)S(1)}, bf16[160,512]{1,0:T(8,128)(2,1)S(1)}, u32[]{:S(2)}, u32[]{:S(2)}) collective-permute-start(bf16[160,512]{1,0:T(8,128)(2,1)S(1)} %slice.8), channel_id=1, source_target_pairs={{0,8},{8,16},{16,24},{24,0},{1,9},{9,17},{17,25},{25,1},{2,10},{10... | collective-permute-start | bytes 491528 | tf_op jit(solution)/shard_map/ppermute | solution.py:328
  69.2 4.6 %collective-permute-start.6 = (bf16[160,512]{1,0:T(8,128)(2,1)S(1)}, bf16[160,512]{1,0:T(8,128)(2,1)S(1)}, u32[]{:S(2)}, u32[]{:S(2)}) collective-permute-start(bf16[160,512]{1,0:T(8,128)(2,1)S(1)} %slice.9), channel_id=1, source_target_pairs={{0,24},{8,0},{16,8},{24,16},{1,25},{9,1},{17,9},{25,17},{2,26},{10... | collective-permute-start | bytes 491528 | tf_op jit(solution)/shard_map/ppermute | solution.py:328
  73.8 1.9 %collective-permute-done.4.refs_2_.w2a = bf16[160,512]{1,0:T(8,128)(2,1)S(1)} collective-permute-done((bf16[160,512]{1,0:T(8,128)(2,1)S(1)}, bf16[160,512]{1,0:T(8,128)(2,1)S(1)}, u32[]{:S(2)}, u32[]{:S(2)}) %collective-permute-start.4) | collective-permute-done | bytes 163872 | tf_op jit(solution)/shard_map/ppermute | solution.py:328
  75.7 1.2 %collective-permute-done.6.refs_3_.w2b = bf16[160,512]{1,0:T(8,128)(2,1)S(1)} collective-permute-done((bf16[160,512]{1,0:T(8,128)(2,1)S(1)}, bf16[160,512]{1,0:T(8,128)(2,1)S(1)}, u32[]{:S(2)}, u32[]{:S(2)}) %collective-permute-start.6) | collective-permute-done | bytes 163872 | tf_op jit(solution)/shard_map/ppermute | solution.py:328
  77.0 0.1 pack_for_core.1
  77.1 0.0 copy-start.2
  77.1 2.1 %collective-permute-start.10 = (bf16[1664,512]{1,0:T(8,128)(2,1)S(1)}, bf16[1664,512]{1,0:T(8,128)(2,1)S(1)}, u32[]{:S(2)}, u32[]{:S(2)}) collective-permute-start(bf16[1664,512]{1,0:T(8,128)(2,1)S(1)} %pack_for_core.1), channel_id=1, source_target_pairs={{0,1},{1,0},{2,3},{3,2},{4,5},{5,4},{6,7},{7,6},{8,9},{9,8},{10,11... | collective-permute-start | bytes 5111816 | tf_op jit(solution)/shard_map/ppermute | solution.py:332
  79.1 3.6 %collective-permute-done.10.other = bf16[1664,512]{1,0:T(8,128)(2,1)S(1)} collective-permute-done((bf16[1664,512]{1,0:T(8,128)(2,1)S(1)}, bf16[1664,512]{1,0:T(8,128)(2,1)S(1)}, u32[]{:S(2)}, u32[]{:S(2)}) %collective-permute-start.10) | collective-permute-done | bytes 1703968 | tf_op jit(solution)/shard_map/ppermute | solution.py:332
  82.7 1.5 %order_rows.1.rows_ref = bf16[256,512]{1,0:T(8,128)(2,1)S(1)} custom-call(s32[5]{0:T(128)S(1)} %stack.23.place, s32[1,256]{1,0:T(1,128)S(1)} %bitcast.13, bf16[192,512]{1,0:T(8,128)(2,1)S(1)} %get-tuple-element.13.refs_5_.f0, bf16[192,512]{1,0:T(8,128)(2,1)S(1)} %collective-permute-done.7.refs_6_.f1, bf16[192,512]{1,0:T(8,128)(2,1)S(1)} %collective-permute-done.8.refs_7_.f2, ...), custom_call_target="tpu_custom_call" | custom-call | tf_op jit(solution)/shard_map/order_rows/pallas_call | solution.py:269
  84.2 0.0 copy-start.7
  84.2 2.1 %project.1 = (f32[256,512]{1,0:T(8,128)S(1)}, bf16[256,512]{1,0:T(8,128)(2,1)S(1)}, f32[256,512]{1,0:T(8,128)S(1)}, bf16[512,512]{1,0:T(8,128)(2,1)S(1)}) custom-call(s32[5]{0:T(128)S(1)} %stack.23.place, bf16[256,512]{1,0:T(8,128)(2,1)S(1)} %bitcast.9, bf16[320,512]{1,0:T(8,128)(2,1)S(1)} %strip_ids.1.refs_0_.w0, ...), custom_call_target="tpu_custom_call" | custom-call | flops 20000000000 | tf_op jit(solution)/shard_map/project/pallas_call | solution.py:230
  86.3 5.6 %all-to-all-done.hist = bf16[64,2,4,1024]{3,2,1,0:T(4,128)(2,1)S(1)} async-done(((bf16[64,2,4,1024]{3,2,1,0:T(4,128)(2,1)}), bf16[64,2,4,1024]{3,2,1,0:T(4,128)(2,1)S(1)}, u32[]{:S(2)}, u32[]{:S(2)}) %all-to-all-start) | async-done | bytes 1048608 | tf_op jit(solution)/shard_map/all_to_all | solution.py:365
  91.9 2.8 %score.1 = f32[2,128]{1,0:T(2,128)} custom-call(s32[2]{0:T(128)S(1)} %copy-done.7, bf16[64,2,4,1024]{3,2,1,0:T(4,128)(2,1)S(1)} %all-to-all-done.hist, bf16[256,512]{1,0:T(8,128)(2,1)S(1)} %get-tuple-element.17.query, f32[256,512]{1,0:T(8,128)S(1)} %get-tuple-element.18.self_term, f32[256,512]{1,0:T(8,128)S(1)} %get-tuple-element.19.gate, ...), custom_call_target="tpu_custom_call" | custom-call | tf_op jit(solution)/shard_map/score/pallas_call | solution.py:316
  (21 shorter events, 0.1 us)
Async XLA Ops:
  0.0 0.8 copy-start.3
  0.8 0.7 copy-start.4
  1.5 34.5 %collective-permute-start = (bf16[40,512]{1,0:T(8,128)(2,1)S(1)}, bf16[40,512]{1,0:T(8,128)(2,1)S(1)}, u32[]{:S(2)}, u32[]{:S(2)}) collective-permute-start(bf16[40,512]{1,0:T(8,128)(2,1)S(1)} %stack_weight_shard.1), channel_id=1, source_target_pairs={{0,0},{1,33},{2,66},{3,99},{4,132},{5,165},{6,198},{7,231},{32,32}... | collective-permute-start | bytes 122888 | tf_op jit(solution)/shard_map/ppermute | solution.py:349
  13.3 22.7 %collective-permute-start.1 = (bf16[40,512]{1,0:T(8,128)(2,1)S(1)}, bf16[40,512]{1,0:T(8,128)(2,1)S(1)}, u32[]{:S(2)}, u32[]{:S(2)}) collective-permute-start(bf16[40,512]{1,0:T(8,128)(2,1)S(1)} %stack_weight_shard.1), channel_id=1, source_target_pairs={{0,256},{1,289},{2,322},{3,355},{4,388},{5,421},{6,454},{7,487},{3... | collective-permute-start | bytes 122888 | tf_op jit(solution)/shard_map/ppermute | solution.py:349
  16.0 19.9 %collective-permute-start.2 = (s32[1,256]{1,0:T(1,128)}, s32[1,256]{1,0:T(1,128)S(1)}, u32[]{:S(2)}, u32[]{:S(2)}) collective-permute-start(s32[1,256]{1,0:T(1,128)} %bitcast.11), channel_id=1, source_target_pairs={{0,1},{1,0},{2,3},{3,2},{4,5},{5,4},{6,7},{7,6},{8,9},{9,8},{10,11... | collective-permute-start | bytes 3080 | tf_op jit(solution)/shard_map/ppermute | solution.py:332
  19.1 1.2 %copy-start = (bf16[128,4,1,1024]{3,1,2,0:T(4,128)(2,1)S(1)}, bf16[128,4,1,1024]{3,1,2,0:T(4,128)(2,1)}, u32[]{:S(2)}) copy-start(bf16[128,4,1,1024]{3,1,2,0:T(4,128)(2,1)} %param.11) | copy-start | bytes 3145732
  20.4 0.7 copy-start.5
  21.1 14.9 %copy-start.6 = (s32[2,128]{1,0:T(2,128)S(1)}, s32[2,128]{1,0:T(2,128)}, u32[]{:S(2)}) copy-start(s32[2,128]{1,0:T(2,128)} %param.14) | copy-start | bytes 3076
  23.0 32.8 %copy-start.1 = (bf16[1024,512]{1,0:T(8,128)(2,1)S(1)}, bf16[1024,512]{1,0:T(8,128)(2,1)}, u32[]{:S(2)}) copy-start(bf16[1024,512]{1,0:T(8,128)(2,1)} %table.1) | copy-start | bytes 3145732
  23.0 68.9 %all-to-all-start = ((bf16[64,2,4,1024]{3,2,1,0:T(4,128)(2,1)}), bf16[64,2,4,1024]{3,2,1,0:T(4,128)(2,1)S(1)}, u32[]{:S(2)}, u32[]{:S(2)}) async-start(bf16[64,2,4,1024]{3,2,1,0:T(4,128)(2,1)} %pick_history.1), calls=%async_computation | async-start | bytes 2097152 | tf_op jit(solution)/shard_map/all_to_all | solution.py:365
  48.7 18.0 %collective-permute-start.3 = (bf16[320,512]{1,0:T(8,128)(2,1)S(1)}, bf16[320,512]{1,0:T(8,128)(2,1)S(1)}, u32[]{:S(2)}, u32[]{:S(2)}) collective-permute-start(bf16[320,512]{1,0:T(8,128)(2,1)S(1)} %strip_ids.1.refs_0_.w0), channel_id=1, source_target_pairs={{0,8},{8,16},{16,24},{24,0},{1,9},{9,17},{17,25},{25,1},{2,10},{10... | collective-permute-start | bytes 983048 | tf_op jit(solution)/shard_map/ppermute | solution.py:328
  52.4 16.8 %collective-permute-start.5 = (bf16[320,512]{1,0:T(8,128)(2,1)S(1)}, bf16[320,512]{1,0:T(8,128)(2,1)S(1)}, u32[]{:S(2)}, u32[]{:S(2)}) collective-permute-start(bf16[320,512]{1,0:T(8,128)(2,1)S(1)} %strip_ids.1.refs_0_.w0), channel_id=1, source_target_pairs={{0,24},{8,0},{16,8},{24,16},{1,25},{9,1},{17,9},{25,17},{2,26},{10... | collective-permute-start | bytes 983048 | tf_op jit(solution)/shard_map/ppermute | solution.py:328
  58.0 15.8 %collective-permute-start.7 = (bf16[192,512]{1,0:T(8,128)(2,1)S(1)}, bf16[192,512]{1,0:T(8,128)(2,1)S(1)}, u32[]{:S(2)}, u32[]{:S(2)}) collective-permute-start(bf16[192,512]{1,0:T(8,128)(2,1)S(1)} %get-tuple-element.14), channel_id=1, source_target_pairs={{0,2},{2,4},{4,6},{6,0},{1,3},{3,5},{5,7},{7,1},{8,10},{10,12},{12... | collective-permute-start | bytes 589832 | tf_op jit(solution)/shard_map/ppermute | solution.py:328
  60.8 13.1 %collective-permute-start.8 = (bf16[192,512]{1,0:T(8,128)(2,1)S(1)}, bf16[192,512]{1,0:T(8,128)(2,1)S(1)}, u32[]{:S(2)}, u32[]{:S(2)}) collective-permute-start(bf16[192,512]{1,0:T(8,128)(2,1)S(1)} %get-tuple-element.15), channel_id=1, source_target_pairs={{0,4},{2,6},{4,0},{6,2},{1,5},{3,7},{5,1},{7,3},{8,12},{10,14},{12... | collective-permute-start | bytes 589832 | tf_op jit(solution)/shard_map/ppermute | solution.py:328
  63.5 10.3 %collective-permute-start.9 = (bf16[192,512]{1,0:T(8,128)(2,1)S(1)}, bf16[192,512]{1,0:T(8,128)(2,1)S(1)}, u32[]{:S(2)}, u32[]{:S(2)}) collective-permute-start(bf16[192,512]{1,0:T(8,128)(2,1)S(1)} %get-tuple-element.16), channel_id=1, source_target_pairs={{0,6},{2,0},{4,2},{6,4},{1,7},{3,1},{5,3},{7,5},{8,14},{10,8},{12,... | collective-permute-start | bytes 589832 | tf_op jit(solution)/shard_map/ppermute | solution.py:328
  66.7 9.0 %collective-permute-start.4 = (bf16[160,512]{1,0:T(8,128)(2,1)S(1)}, bf16[160,512]{1,0:T(8,128)(2,1)S(1)}, u32[]{:S(2)}, u32[]{:S(2)}) collective-permute-start(bf16[160,512]{1,0:T(8,128)(2,1)S(1)} %slice.8), channel_id=1, source_target_pairs={{0,8},{8,16},{16,24},{24,0},{1,9},{9,17},{17,25},{25,1},{2,10},{10... | collective-permute-start | bytes 491528 | tf_op jit(solution)/shard_map/ppermute | solution.py:328
  69.2 7.7 %collective-permute-start.6 = (bf16[160,512]{1,0:T(8,128)(2,1)S(1)}, bf16[160,512]{1,0:T(8,128)(2,1)S(1)}, u32[]{:S(2)}, u32[]{:S(2)}) collective-permute-start(bf16[160,512]{1,0:T(8,128)(2,1)S(1)} %slice.9), channel_id=1, source_target_pairs={{0,24},{8,0},{16,8},{24,16},{1,25},{9,1},{17,9},{25,17},{2,26},{10... | collective-permute-start | bytes 491528 | tf_op jit(solution)/shard_map/ppermute | solution.py:328
  77.1 7.1 %copy-start.2 = (bf16[2,128,512]{2,1,0:T(8,128)(2,1)S(1)}, bf16[2,128,512]{2,1,0:T(8,128)(2,1)}, u32[]{:S(2)}) copy-start(bf16[2,128,512]{2,1,0:T(8,128)(2,1)} %param.8) | copy-start | bytes 786436
  77.1 5.6 %collective-permute-start.10 = (bf16[1664,512]{1,0:T(8,128)(2,1)S(1)}, bf16[1664,512]{1,0:T(8,128)(2,1)S(1)}, u32[]{:S(2)}, u32[]{:S(2)}) collective-permute-start(bf16[1664,512]{1,0:T(8,128)(2,1)S(1)} %pack_for_core.1), channel_id=1, source_target_pairs={{0,1},{1,0},{2,3},{3,2},{4,5},{5,4},{6,7},{7,6},{8,9},{9,8},{10,11... | collective-permute-start | bytes 5111816 | tf_op jit(solution)/shard_map/ppermute | solution.py:332
  84.2 7.7 %copy-start.7 = (s32[2]{0:T(128)S(1)}, s32[2]{0:T(128)}, u32[]{:S(2)}) copy-start(s32[2]{0:T(128)} %lengths.1) | copy-start | bytes 28

commit v3 on v2

--- a/solution.py
+++ b/solution.py
@@ -14,6 +14,7 @@
 VMEM = pltpu.VMEM
 SMEM = pltpu.SMEM
 VMEM_LIMIT = 40 * 1024 * 1024
+PICK_LIMIT = 60 * 1024 * 1024
 
 USER = ("z", "y")
 ITEM = ("x", "core")
@@ -24,7 +25,8 @@
 
 
 def silu(values):
-    return values * jax.nn.sigmoid(values)
+    half = 0.5 * values
+    return half + half * jnp.tanh(half)
 
 
 def iota(shape, dim):
@@ -33,26 +35,6 @@
 
 def dot(a, b):
     return jnp.dot(a, b, preferred_element_type=F32)
-
-
-def shard_kernel(proj_weight, out_weight, out):
-    width = out.shape[1]
-    wide = proj_weight[...].astype(F32)
-    parts = [wide[:, k * width : (k + 1) * width] for k in range(4)]
-    parts.append(out_weight[...].astype(F32))
-    out[...] = jnp.concatenate(parts, axis=0).astype(BF16)
-
-
-def stack_shard(proj_weight, out_weight):
-    rows, width = out_weight.shape
-    return pl.pallas_call(
-        shard_kernel,
-        out_shape=jax.ShapeDtypeStruct((rows * 5, width), BF16),
-        in_specs=[pl.BlockSpec(memory_space=VMEM)] * 2,
-        out_specs=pl.BlockSpec(memory_space=VMEM),
-        compiler_params=params(),
-        name="stack_weight_shard",
-    )(proj_weight, out_weight)
 
 
 def block_kernel(p0, p1, my_ids, other_ids, out):
@@ -79,10 +61,14 @@
     )(p0, p1, my_ids, other_ids)
 
 
-def pick_kernel(slots, place, hist, out):
+def pick_kernel(slots, place, proj_weight, out_weight, hist, shard, out):
+    width = shard.shape[1]
+    wide = proj_weight[...].astype(F32)
+    parts = [wide[:, k * width : (k + 1) * width] for k in range(4)]
+    parts.append(out_weight[...].astype(F32))
+    shard[...] = jnp.concatenate(parts, axis=0).astype(BF16)
     item = place[0]
-    owners = out.shape[0]
-    users = out.shape[1]
+    owners, users = out.shape[0], out.shape[1]
     group = hist.shape[0]
 
     def one(owner, carry):
@@ -91,22 +77,37 @@
             out[owner, slot] = hist[local]
         return carry
 
-    lax.fori_loop(0, owners, one, 0, unroll=4)
-
-
-def pick(scorer_user, place, hist, owners, users):
+    lax.fori_loop(0, owners, one, 0, unroll=8)
+
+
+def pick(scorer_user, place, proj_weight, out_weight, hist, owners, users):
+    rows, width = out_weight.shape
     return pl.pallas_call(
         pick_kernel,
-        out_shape=jax.ShapeDtypeStruct((owners, users) + hist.shape[1:], hist.dtype),
-        in_specs=[
-            pl.BlockSpec(memory_space=SMEM),
-            pl.BlockSpec(memory_space=SMEM),
-            pl.BlockSpec(memory_space=VMEM),
-        ],
+        out_shape=(
+            jax.ShapeDtypeStruct((rows * 5, width), BF16),
+            jax.ShapeDtypeStruct((owners, users) + hist.shape[1:], hist.dtype),
+        ),
+        in_specs=[pl.BlockSpec(memory_space=SMEM)] * 2 + [pl.BlockSpec(memory_space=VMEM)] * 3,
+        out_specs=(pl.BlockSpec(memory_space=VMEM),) * 2,
+        compiler_params=pltpu.CompilerParams(vmem_limit_bytes=PICK_LIMIT),
+        name="stack_and_pick",
+    )(scorer_user, place, proj_weight, out_weight, hist)
+
+
+def later_kernel(first, values, out):
+    out[...] = values[...]
+
+
+def later(first, values):
+    return pl.pallas_call(
+        later_kernel,
+        out_shape=jax.ShapeDtypeStruct(values.shape, values.dtype),
+        in_specs=[pl.BlockSpec(memory_space=pl.ANY), pl.BlockSpec(memory_space=VMEM)],
         out_specs=pl.BlockSpec(memory_space=VMEM),
         compiler_params=params(),
-        name="pick_history",
-    )(scorer_user, place, hist)
+        name="ids_later",
+    )(first, values)
 
 
 def fetch_kernel(place, gathered, table, *outs):
@@ -184,21 +185,44 @@
     )(*pieces)
 
 
-def proj_kernel(
-    place, cand, w0, w1, w2a, w2b, w3, other, gate, query, self_term, out_weight
+def natural_rows(place, half, size):
+    g = iota((size, size // 2), 1)
+    peer = (g // 16) % 4 * 2 + (place[2] + half) % 2
+    from_z = (place[4] + 32 - peer - (g // 8) % 2 * 8) % 16
+    from_y = (place[3] + 4 - (g // 64) % 4) % 4
+    natural = from_z * 32 + from_y * 8 + g % 8
+    return (iota((size, size // 2), 0) == natural).astype(BF16)
+
+
+def row_keys(place, ids):
+    rows = ids.shape[1]
+    shard = ids // 1024
+    before = (iota((rows, rows), 0) < iota((rows, rows), 1)).astype(BF16)
+    hot = iota((8, rows), 0) == shard
+    ranks = dot(hot.astype(BF16), before)
+    rank = jnp.sum(jnp.where(hot, ranks, 0.0), axis=0, keepdims=True)
+    offset = ((place[1] + 4 - shard // 2) % 4) * 2 + (place[2] + 2 - shard % 2) % 2
+    return rank, offset
+
+
+def place_rows(rank, offset, at, piece):
+    key = jnp.where(offset == at, rank, -1.0)
+    chosen = (iota((CAP, rank.shape[1]), 0).astype(F32) == key).astype(BF16)
+    return lax.dot_general(
+        chosen, piece, (((0,), (0,)), ((), ())), preferred_element_type=F32
+    )
+
+
+def own_kernel(
+    place, ids, cand, w0, w1, w2a, w2b, w3, f0, f1, f2, f3, part, rest, out_weight, rows_out
 ):
-    core = place[2]
-    rows, width = cand.shape
+    width = cand.shape[1]
     values = cand[...].astype(F32)
     center = values - jnp.mean(values, axis=-1, keepdims=True)
     spread = jnp.mean(center * center, axis=-1, keepdims=True)
     normed = (center * lax.rsqrt(spread + 1e-06)).astype(BF16)
-    g = iota((width, width), 1)
-    peer = (g // 16) % 4 * 2 + (core + g // 256) % 2
-    from_z = (place[4] + 32 - peer - (g // 8) % 2 * 8) % 16
-    from_y = (place[3] + 4 - (g // 64) % 4) % 4
-    natural = from_z * 32 + from_y * 8 + g % 8
-    perm = (iota((width, width), 0) == natural).astype(BF16)
+    rest[...] = dot(normed, natural_rows(place, 1, width)).astype(BF16)
+    perm = natural_rows(place, 0, width)
     normed = dot(normed, perm).astype(BF16)
     shard = w0.shape[0]
 
@@ -208,14 +232,54 @@
         own += [(w2a, parts[0]), (w2a, parts[1])]
         own += [(w2b, parts[2] - shard // 2), (w2b, parts[3] - shard // 2)]
         own += [(w3, at) for at in parts]
-        own += [(other, k * shard + at) for k in range(4) for at in parts]
         return jnp.concatenate([ref[at : at + 16] for ref, at in own], axis=0)
 
     out_weight[...] = dot(perm, weight(4)).astype(BF16)
-    gate[...] = silu(dot(normed, weight(0)))
-    value = silu(dot(normed, weight(1))).astype(BF16).astype(F32)
-    q = silu(dot(normed, weight(2))).astype(BF16)
-    k = silu(dot(normed, weight(3))).astype(BF16)
+    for k in range(4):
+        part[:, k * width : (k + 1) * width] = dot(normed, weight(k))
+    rank, offset = row_keys(place, ids[...])
+    total = place_rows(rank, offset, 0, f0[:CAP]) + place_rows(rank, offset, 2, f1[:CAP])
+    total += place_rows(rank, offset, 4, f2[:CAP]) + place_rows(rank, offset, 6, f3[:CAP])
+    rows_out[...] = total.astype(BF16)
+
+
+def project_own(place, ids, cand, pieces, found):
+    rows, width = cand.shape
+    return pl.pallas_call(
+        own_kernel,
+        out_shape=(
+            jax.ShapeDtypeStruct((rows, 4 * width), F32),
+            jax.ShapeDtypeStruct((rows, width // 2), BF16),
+            jax.ShapeDtypeStruct((width, width), BF16),
+            jax.ShapeDtypeStruct((rows, width), BF16),
+        ),
+        in_specs=[pl.BlockSpec(memory_space=SMEM)] + [pl.BlockSpec(memory_space=VMEM)] * 11,
+        out_specs=(pl.BlockSpec(memory_space=VMEM),) * 4,
+        compiler_params=params(),
+        name="project_own",
+    )(place, ids, cand, *pieces, *found)
+
+
+def rest_kernel(
+    place, ids, part, rest, own_weight, own_rows, other, gate, query, self_term, out_weight, rows_out
+):
+    width = own_rows.shape[1]
+    shard = (other.shape[0] - 4 * CAP) // 4
+    normed = rest[...]
+
+    def weight(cols):
+        parts = [k * shard + (x * 5 + cols) * 16 for k in range(4) for x in range(4)]
+        return jnp.concatenate([other[at : at + 16] for at in parts], axis=0)
+
+    def proj(k):
+        return silu(part[:, k * width : (k + 1) * width] + dot(normed, weight(k)))
+
+    perm = natural_rows(place, 1, width)
+    out_weight[...] = own_weight[...] + dot(perm, weight(4)).astype(BF16)
+    gate[...] = proj(0)
+    value = proj(1).astype(BF16).astype(F32)
+    q = proj(2).astype(BF16)
+    k = proj(3).astype(BF16)
     query[...] = q
     product = q.astype(F32) * k.astype(F32)
     head = width // HEADS
@@ -223,57 +287,31 @@
         cols = slice(h * head, (h + 1) * head)
         score = jnp.sum(product[:, cols], axis=-1, keepdims=True) * head ** (-0.5)
         self_term[:, cols] = silu(score).astype(BF16).astype(F32) * value[:, cols]
-
-
-def project(place, cand, pieces, other):
-    rows, width = cand.shape
-    return pl.pallas_call(
-        proj_kernel,
+    rank, offset = row_keys(place, ids[...])
+    total = own_rows[...].astype(F32)
+    for k in range(4):
+        at = other.shape[0] - (4 - k) * CAP
+        total += place_rows(rank, offset, 2 * k + 1, other[at : at + CAP])
+    rows_out[...] = total.astype(BF16)
+
+
+def project_rest(place, ids, own, other):
+    rows, width = own[3].shape
+    return pl.pallas_call(
+        rest_kernel,
         out_shape=(
             jax.ShapeDtypeStruct((rows, width), F32),
             jax.ShapeDtypeStruct((rows, width), BF16),
             jax.ShapeDtypeStruct((rows, width), F32),
             jax.ShapeDtypeStruct((width, width), BF16),
+            jax.ShapeDtypeStruct((rows, width), BF16),
         ),
-        in_specs=[pl.BlockSpec(memory_space=SMEM)] + [pl.BlockSpec(memory_space=VMEM)] * 7,
-        out_specs=(pl.BlockSpec(memory_space=VMEM),) * 4,
+        in_specs=[pl.BlockSpec(memory_space=SMEM)] + [pl.BlockSpec(memory_space=VMEM)] * 6,
+        out_specs=(pl.BlockSpec(memory_space=VMEM),) * 5,
         compiler_params=params(),
         name="project",
-        cost_estimate=pl.CostEstimate(flops=int(2e10), bytes_accessed=0, transcendentals=0),
-    )(place, cand, *pieces, other)
-
-
-def order_kernel(place, ids, f0, f1, f2, f3, other, out):
-    own = (f0, f1, f2, f3)
-    x, core = place[1], place[2]
-    rows, width = out.shape
-    shard = ids[...] // 1024
-    before = (iota((rows, rows), 0) < iota((rows, rows), 1)).astype(BF16)
-    hot = iota((8, rows), 0) == shard
-    ranks = dot(hot.astype(BF16), before)
-    rank = jnp.sum(jnp.where(hot, ranks, 0.0), axis=0, keepdims=True)
-    offset = ((x + 4 - shard // 2) % 4) * 2 + (core + 2 - shard % 2) % 2
-    total = jnp.zeros((rows, width), F32)
-    for j in range(8):
-        key = jnp.where(offset == j, rank, -1.0)
-        chosen = (iota((CAP, rows), 0).astype(F32) == key).astype(BF16)
-        at = other.shape[0] - (4 - j // 2) * CAP
-        piece = other[at : at + CAP] if j % 2 else own[j // 2][:CAP]
-        total += lax.dot_general(
-            chosen, piece, (((0,), (0,)), ((), ())), preferred_element_type=F32
-        )
-    out[...] = total.astype(BF16)
-
-
-def order(place, ids, pieces, other):
-    return pl.pallas_call(
-        order_kernel,
-        out_shape=jax.ShapeDtypeStruct((ids.shape[1], other.shape[1]), BF16),
-        in_specs=[pl.BlockSpec(memory_space=SMEM)] + [pl.BlockSpec(memory_space=VMEM)] * 6,
-        out_specs=pl.BlockSpec(memory_space=VMEM),
-        compiler_params=params(),
-        name="order_rows",
-    )(place, ids, *pieces, other)
+        cost_estimate=pl.CostEstimate(flops=int(1.9e10), bytes_accessed=0, transcendentals=0),
+    )(place, ids, *own, other)
 
 
 def score_kernel(lengths, hist, query, self_term, gate, cand, out_weight, rows_ref, out):
@@ -297,8 +335,8 @@
             ) * (head ** (-0.5))
             weights = jnp.where(live, silu(scores), 0.0).astype(BF16)
             parts.append(dot(weights, kv[:, width + h * head : width + (h + 1) * head]))
-        attended = (jnp.concatenate(parts, axis=1) + self_term[at]) / (
-            length.astype(F32) + 1.0
+        attended = (jnp.concatenate(parts, axis=1) + self_term[at]) * (
+            1.0 / (length.astype(F32) + 1.0)
         )
         center = attended - jnp.mean(attended, axis=-1, keepdims=True)
         spread = jnp.mean(center * center, axis=-1, keepdims=True)
@@ -343,7 +381,9 @@
     place = jnp.stack([item, x, core, y, z]).astype(jnp.int32)
     owners = lax.axis_size(USER)
 
-    shard = stack_shard(proj_weight, out_weight)
+    hist = history_kv.reshape(history_kv.shape[0], history_kv.shape[1], -1)
+    shard, picked = pick(scorer_user, place, proj_weight, out_weight, hist, owners, users)
+
     zs, items = lax.axis_size("z"), lax.axis_size(ITEM)
     shards = [
         lax.ppermute(
@@ -357,12 +397,11 @@
         )
         for step in (8, 0)
     ][::-1]
+
+    arrived = lax.all_to_all(picked, USER, split_axis=0, concat_axis=0, tiled=True)
+
     my_ids = cand_item.reshape(1, users * count)
-    other_ids = swap_core(my_ids)
-
-    hist = history_kv.reshape(history_kv.shape[0], history_kv.shape[1], -1)
-    picked = pick(scorer_user, place, hist, owners, users)
-    arrived = lax.all_to_all(picked, USER, split_axis=0, concat_axis=0, tiled=True)
+    other_ids = swap_core(later(picked, my_ids))
 
     gathered = lax.all_gather(block(*shards, my_ids, other_ids), "x", axis=0, tiled=True)
     weight = strip(gathered)
@@ -375,8 +414,8 @@
     for k in (1, 3, 2):
         found[k] = along("x", found[k], k)
     other = swap_core(pack((0,) * 5 + (CAP,) * 4, pieces + found))
-    gate, query, self_term, out_w = project(place, cand, pieces, other)
-    rows = order(place, my_ids, found, other)
+    own = project_own(place, my_ids, cand, pieces, found)
+    gate, query, self_term, out_w, rows = project_rest(place, my_ids, own, other)
     return score(hist_len, arrived, query, self_term, gate, cand, out_w, rows)
 
 

time: 95.4 us -> 92.6 us (0.971)
  the two profiles are of different devices: /device:TPU:6 before, /device:TPU:1 now
where the time goes in v3:
time: 92.6 us; the launch traced here: 92 us
  starting transfers between devices  57.2 us (62%)
  blocking collectives  13.5 us (15%)
  Pallas kernels  11.7 us (13%)
  waiting for transfers between devices  8.58 us (9%)
    ppermute x7, starting transfers between devices, along(): lax.ppermute(values, axis, [(j, (j + offset) % size) for j in range(size)])  21.8 us
    ppermute x2, starting transfers between devices, body(): lax.ppermute(shard, ('z',) + ITEM, [(k * items + i, (k + i + step) % zs *...  18.6 us
    all_gather x1, blocking collectives, body(): lax.all_gather(block(*shards, my_ids, other_ids), 'x', axis=0, tiled=True)  13.5 us
    ppermute x2, starting transfers between devices, swap_core(): return lax.ppermute(values, 'core', [(0, 1), (1, 0)])  9.35 us
    all_to_all x1, starting transfers between devices, body(): lax.all_to_all(picked, USER, split_axis=0, concat_axis=0, tiled=True)  7.49 us
    ppermute x7, waiting for transfers between devices, along(): lax.ppermute(values, axis, [(j, (j + offset) % size) for j in range(size)])  6.54 us
    pallas_call x1, Pallas kernels, score(): pl.pallas_call(score_kernel, out_shape=jax.ShapeDtypeStruct((users, cand....  2.84 us
    pallas_call x1, Pallas kernels, pick(): pl.pallas_call(pick_kernel, out_shape=(jax.ShapeDtypeStruct((rows * 5, wi...  2.53 us
  transfers between devices with their start and end apart: 12, of which 4 were waited for; matrix products, arithmetic and copies ran while one was open for 0% of the time, Pallas kernels for 7%

profile of v3, /device:TPU:1, one launch (start us, length us, event | category | flops | bytes accessed | tf_op | source)
XLA Modules:
  0.0 92.0 jit_solution(4166666956829788291)
XLA Ops:
  0.0 0.6 stack.23.place
  0.6 2.5 %stack_and_pick.1 = (bf16[40,512]{1,0:T(8,128)(2,1)}, bf16[64,2,4,1024]{3,2,1,0:T(4,128)(2,1)}) custom-call(s32[1024]{0:T(1024)} %slots.1, s32[5]{0:T(128)} %stack.23.place, bf16[8,2048]{1,0:T(8,128)(2,1)} %proj_weight.1, bf16[8,512]{1,0:T(8,128)(2,1)} %out_weight.1, bf16[128,4,1024]{2,1,0:T(4,128)(2,1)} %bitcast.14), custom_call_target="tpu_custom_call" | custom-call | tf_op jit(solution)/shard_map/stack_and_pick/pallas_call | solution.py:85
  3.2 15.9 %collective-permute-start.1 = (bf16[40,512]{1,0:T(8,128)(2,1)}, bf16[40,512]{1,0:T(8,128)(2,1)S(1)}, u32[]{:S(2)}, u32[]{:S(2)}) collective-permute-start(bf16[40,512]{1,0:T(8,128)(2,1)} %get-tuple-element.21), channel_id=1, source_target_pairs={{0,256},{1,289},{2,322},{3,355},{4,388},{5,421},{6,454},{7,487},{3... | collective-permute-start | bytes 122888 | tf_op jit(solution)/shard_map/ppermute | solution.py:389
  19.1 2.6 %collective-permute-start = (bf16[40,512]{1,0:T(8,128)(2,1)}, bf16[40,512]{1,0:T(8,128)(2,1)S(1)}, u32[]{:S(2)}, u32[]{:S(2)}) collective-permute-start(bf16[40,512]{1,0:T(8,128)(2,1)} %get-tuple-element.21), channel_id=1, source_target_pairs={{0,0},{1,33},{2,66},{3,99},{4,132},{5,165},{6,198},{7,231},{32,32}... | collective-permute-start | bytes 122888 | tf_op jit(solution)/shard_map/ppermute | solution.py:389
  21.8 7.5 %all-to-all-start = ((bf16[64,2,4,1024]{3,2,1,0:T(4,128)(2,1)}), bf16[64,2,4,1024]{3,2,1,0:T(4,128)(2,1)S(1)}, u32[]{:S(2)}, u32[]{:S(2)}) async-start(bf16[64,2,4,1024]{3,2,1,0:T(4,128)(2,1)} %get-tuple-element.20.first), calls=%async_computation | async-start | bytes 2097152 | tf_op jit(solution)/shard_map/all_to_all | solution.py:401
  29.3 0.0 copy-start.1
  29.3 3.4 %collective-permute-start.2 = (s32[1,256]{1,0:T(1,128)S(1)}, s32[1,256]{1,0:T(1,128)S(1)}, u32[]{:S(2)}, u32[]{:S(2)}) collective-permute-start(s32[1,256]{1,0:T(1,128)S(1)} %ids_later.1), channel_id=1, source_target_pairs={{0,1},{1,0},{2,3},{3,2},{4,5},{5,4},{6,7},{7,6},{8,9},{9,8},{10,11... | collective-permute-start | bytes 3080 | tf_op jit(solution)/shard_map/ppermute | solution.py:370
  32.7 0.8 collective-permute-done.2.other_ids
  33.5 0.0 collective-permute-done.1.p1
  33.5 0.0 collective-permute-done.p0
  33.5 0.1 block_weights_and_ids.1
  33.7 13.5 %all_gather.3.gathered = bf16[384,512]{1,0:T(8,128)(2,1)S(1)} all-gather(bf16[96,512]{1,0:T(8,128)(2,1)S(1)} %block_weights_and_ids.1), channel_id=1, replica_groups=mesh['z'=16,'y'=4,'x'=4,'core'=2] {'x'}, dimensions={0}, use_global_device_ids=true | all-gather | bytes 491520 | tf_op jit(solution)/shard_map/all_gather | solution.py:406
  47.2 4.4 %collective-permute-start.5 = (bf16[320,512]{1,0:T(8,128)(2,1)S(1)}, bf16[320,512]{1,0:T(8,128)(2,1)S(1)}, u32[]{:S(2)}, u32[]{:S(2)}) collective-permute-start(bf16[320,512]{1,0:T(8,128)(2,1)S(1)} %strip_ids.1.w0.refs_0_), channel_id=1, source_target_pairs={{0,24},{8,0},{16,8},{24,16},{1,25},{9,1},{17,9},{25,17},{2,26},{10... | collective-permute-start | bytes 983048 | tf_op jit(solution)/shard_map/ppermute | solution.py:366
  51.7 1.9 %collective-permute-start.3 = (bf16[320,512]{1,0:T(8,128)(2,1)S(1)}, bf16[320,512]{1,0:T(8,128)(2,1)S(1)}, u32[]{:S(2)}, u32[]{:S(2)}) collective-permute-start(bf16[320,512]{1,0:T(8,128)(2,1)S(1)} %strip_ids.1.w0.refs_0_), channel_id=1, source_target_pairs={{0,8},{8,16},{16,24},{24,0},{1,9},{9,17},{17,25},{25,1},{2,10},{10... | collective-permute-start | bytes 983048 | tf_op jit(solution)/shard_map/ppermute | solution.py:366
  53.6 2.3 %fetch_rows.1 = (bf16[192,512]{1,0:T(8,128)(2,1)S(1)}, bf16[192,512]{1,0:T(8,128)(2,1)S(1)}, bf16[192,512]{1,0:T(8,128)(2,1)S(1)}, bf16[192,512]{1,0:T(8,128)(2,1)S(1)}) custom-call(s32[5]{0:T(128)S(1)} %copy-done.4, bf16[384,512]{1,0:T(8,128)(2,1)S(1)} %all_gather.3.gathered, bf16[1024,512]{1,0:T(8,128)(2,1)S(1)} %copy-done.1), custom_call_target="tpu_custom_call" | custom-call | tf_op jit(solution)/shard_map/fetch_rows/pallas_call | solution.py:139
  55.9 2.4 %collective-permute-start.7 = (bf16[192,512]{1,0:T(8,128)(2,1)S(1)}, bf16[192,512]{1,0:T(8,128)(2,1)S(1)}, u32[]{:S(2)}, u32[]{:S(2)}) collective-permute-start(bf16[192,512]{1,0:T(8,128)(2,1)S(1)} %get-tuple-element.23), channel_id=1, source_target_pairs={{0,2},{2,4},{4,6},{6,0},{1,3},{3,5},{5,7},{7,1},{8,10},{10,12},{12... | collective-permute-start | bytes 589832 | tf_op jit(solution)/shard_map/ppermute | solution.py:366
  58.3 4.3 %collective-permute-start.8 = (bf16[192,512]{1,0:T(8,128)(2,1)S(1)}, bf16[192,512]{1,0:T(8,128)(2,1)S(1)}, u32[]{:S(2)}, u32[]{:S(2)}) collective-permute-start(bf16[192,512]{1,0:T(8,128)(2,1)S(1)} %get-tuple-element.24), channel_id=1, source_target_pairs={{0,4},{2,6},{4,0},{6,2},{1,5},{3,7},{5,1},{7,3},{8,12},{10,14},{12... | collective-permute-start | bytes 589832 | tf_op jit(solution)/shard_map/ppermute | solution.py:366
  62.6 2.3 %collective-permute-start.9 = (bf16[192,512]{1,0:T(8,128)(2,1)S(1)}, bf16[192,512]{1,0:T(8,128)(2,1)S(1)}, u32[]{:S(2)}, u32[]{:S(2)}) collective-permute-start(bf16[192,512]{1,0:T(8,128)(2,1)S(1)} %get-tuple-element.25), channel_id=1, source_target_pairs={{0,6},{2,0},{4,2},{6,4},{1,7},{3,1},{5,3},{7,5},{8,14},{10,8},{12,... | collective-permute-start | bytes 589832 | tf_op jit(solution)/shard_map/ppermute | solution.py:366
  64.9 0.0 collective-permute-done.5.w3.refs_4_
  64.9 4.6 %collective-permute-start.6 = (bf16[160,512]{1,0:T(8,128)(2,1)S(1)}, bf16[160,512]{1,0:T(8,128)(2,1)S(1)}, u32[]{:S(2)}, u32[]{:S(2)}) collective-permute-start(bf16[160,512]{1,0:T(8,128)(2,1)S(1)} %slice.9), channel_id=1, source_target_pairs={{0,24},{8,0},{16,8},{24,16},{1,25},{9,1},{17,9},{25,17},{2,26},{10... | collective-permute-start | bytes 491528 | tf_op jit(solution)/shard_map/ppermute | solution.py:366
  69.5 0.0 collective-permute-done.3.w1.refs_1_
  69.5 1.9 %collective-permute-start.4 = (bf16[160,512]{1,0:T(8,128)(2,1)S(1)}, bf16[160,512]{1,0:T(8,128)(2,1)S(1)}, u32[]{:S(2)}, u32[]{:S(2)}) collective-permute-start(bf16[160,512]{1,0:T(8,128)(2,1)S(1)} %slice.8), channel_id=1, source_target_pairs={{0,8},{8,16},{16,24},{24,0},{1,9},{9,17},{17,25},{25,1},{2,10},{10... | collective-permute-start | bytes 491528 | tf_op jit(solution)/shard_map/ppermute | solution.py:366
  71.5 0.0 collective-permute-done.8.f2.refs_7_
  71.5 1.1 %collective-permute-done.6.w2b.refs_3_ = bf16[160,512]{1,0:T(8,128)(2,1)S(1)} collective-permute-done((bf16[160,512]{1,0:T(8,128)(2,1)S(1)}, bf16[160,512]{1,0:T(8,128)(2,1)S(1)}, u32[]{:S(2)}, u32[]{:S(2)}) %collective-permute-start.6) | collective-permute-done | bytes 163872 | tf_op jit(solution)/shard_map/ppermute | solution.py:366
  72.6 5.5 %collective-permute-done.4.w2a.refs_2_ = bf16[160,512]{1,0:T(8,128)(2,1)S(1)} collective-permute-done((bf16[160,512]{1,0:T(8,128)(2,1)S(1)}, bf16[160,512]{1,0:T(8,128)(2,1)S(1)}, u32[]{:S(2)}, u32[]{:S(2)}) %collective-permute-start.4) | collective-permute-done | bytes 163872 | tf_op jit(solution)/shard_map/ppermute | solution.py:366
  78.0 0.1 pack_for_core.1
  78.1 6.0 %collective-permute-start.10 = (bf16[1664,512]{1,0:T(8,128)(2,1)S(1)}, bf16[1664,512]{1,0:T(8,128)(2,1)S(1)}, u32[]{:S(2)}, u32[]{:S(2)}) collective-permute-start(bf16[1664,512]{1,0:T(8,128)(2,1)S(1)} %pack_for_core.1), channel_id=1, source_target_pairs={{0,1},{1,0},{2,3},{3,2},{4,5},{5,4},{6,7},{7,6},{8,9},{9,8},{10,11... | collective-permute-start | bytes 5111816 | tf_op jit(solution)/shard_map/ppermute | solution.py:370
  84.1 1.9 %project_own.1 = (f32[256,2048]{1,0:T(8,128)S(1)}, bf16[256,256]{1,0:T(8,128)(2,1)S(1)}, bf16[512,512]{1,0:T(8,128)(2,1)S(1)}, bf16[256,512]{1,0:T(8,128)(2,1)S(1)}) custom-call(s32[5]{0:T(128)S(1)} %copy-done.4, s32[1,256]{1,0:T(1,128)S(1)} %bitcast.12, bf16[256,512]{1,0:T(8,128)(2,1)S(1)} %bitcast.8, bf16[320,512]{1,0:T(8,128)(2,1)S(1)} %strip_ids.1.w0.refs_0_, ...), custom_call_target="tpu_custom_call" | custom-call | tf_op jit(solution)/shard_map/project_own/pallas_call | solution.py:248
  86.1 1.2 %collective-permute-done.10.other = bf16[1664,512]{1,0:T(8,128)(2,1)S(1)} collective-permute-done((bf16[1664,512]{1,0:T(8,128)(2,1)S(1)}, bf16[1664,512]{1,0:T(8,128)(2,1)S(1)}, u32[]{:S(2)}, u32[]{:S(2)}) %collective-permute-start.10) | collective-permute-done | bytes 1703968 | tf_op jit(solution)/shard_map/ppermute | solution.py:370
  87.3 1.8 %project.1 = (f32[256,512]{1,0:T(8,128)S(1)}, bf16[256,512]{1,0:T(8,128)(2,1)S(1)}, f32[256,512]{1,0:T(8,128)S(1)}, bf16[512,512]{1,0:T(8,128)(2,1)S(1)}, bf16[256,512]{1,0:T(8,128)(2,1)S(1)}) custom-call(s32[5]{0:T(128)S(1)} %copy-done.4, s32[1,256]{1,0:T(1,128)S(1)} %bitcast.13, f32[256,2048]{1,0:T(8,128)S(1)} %get-tuple-element.26.part, ...), custom_call_target="tpu_custom_call" | custom-call | flops 19000000512 | tf_op jit(solution)/shard_map/project/pallas_call | solution.py:300
  89.1 0.0 all-to-all-done.hist
  89.1 2.8 %score.1 = f32[2,128]{1,0:T(2,128)} custom-call(s32[2]{0:T(128)S(1)} %copy-done.5, bf16[64,2,4,1024]{3,2,1,0:T(4,128)(2,1)S(1)} %all-to-all-done.hist, bf16[256,512]{1,0:T(8,128)(2,1)S(1)} %get-tuple-element.30.query, f32[256,512]{1,0:T(8,128)S(1)} %get-tuple-element.31.self_term, f32[256,512]{1,0:T(8,128)S(1)} %get-tuple-element.32.gate, ...), custom_call_target="tpu_custom_call" | custom-call | tf_op jit(solution)/shard_map/score/pallas_call | solution.py:354
  (17 shorter events, 0.1 us)
Async XLA Ops:
  0.0 29.3 %copy-start.3 = (s32[2,128]{1,0:T(2,128)S(1)}, s32[2,128]{1,0:T(2,128)}, u32[]{:S(2)}) copy-start(s32[2,128]{1,0:T(2,128)} %param.14) | copy-start | bytes 3076
  3.1 26.1 %copy-start = (bf16[64,2,4,1024]{3,2,1,0:T(4,128)(2,1)S(1)}, bf16[64,2,4,1024]{3,2,1,0:T(4,128)(2,1)}, u32[]{:S(2)}) copy-start(bf16[64,2,4,1024]{3,2,1,0:T(4,128)(2,1)} %get-tuple-element.20.first) | copy-start | bytes 3145732
  3.2 30.4 %collective-permute-start.1 = (bf16[40,512]{1,0:T(8,128)(2,1)}, bf16[40,512]{1,0:T(8,128)(2,1)S(1)}, u32[]{:S(2)}, u32[]{:S(2)}) collective-permute-start(bf16[40,512]{1,0:T(8,128)(2,1)} %get-tuple-element.21), channel_id=1, source_target_pairs={{0,256},{1,289},{2,322},{3,355},{4,388},{5,421},{6,454},{7,487},{3... | collective-permute-start | bytes 122888 | tf_op jit(solution)/shard_map/ppermute | solution.py:389
  19.1 14.4 %collective-permute-start = (bf16[40,512]{1,0:T(8,128)(2,1)}, bf16[40,512]{1,0:T(8,128)(2,1)S(1)}, u32[]{:S(2)}, u32[]{:S(2)}) collective-permute-start(bf16[40,512]{1,0:T(8,128)(2,1)} %get-tuple-element.21), channel_id=1, source_target_pairs={{0,0},{1,33},{2,66},{3,99},{4,132},{5,165},{6,198},{7,231},{32,32}... | collective-permute-start | bytes 122888 | tf_op jit(solution)/shard_map/ppermute | solution.py:389
  21.8 67.4 %all-to-all-start = ((bf16[64,2,4,1024]{3,2,1,0:T(4,128)(2,1)}), bf16[64,2,4,1024]{3,2,1,0:T(4,128)(2,1)S(1)}, u32[]{:S(2)}, u32[]{:S(2)}) async-start(bf16[64,2,4,1024]{3,2,1,0:T(4,128)(2,1)} %get-tuple-element.20.first), calls=%async_computation | async-start | bytes 2097152 | tf_op jit(solution)/shard_map/all_to_all | solution.py:401
  29.3 24.3 %copy-start.1 = (bf16[1024,512]{1,0:T(8,128)(2,1)S(1)}, bf16[1024,512]{1,0:T(8,128)(2,1)}, u32[]{:S(2)}) copy-start(bf16[1024,512]{1,0:T(8,128)(2,1)} %table.1) | copy-start | bytes 3145732
  29.3 24.3 %copy-start.4 = (s32[5]{0:T(128)S(1)}, s32[5]{0:T(128)}, u32[]{:S(2)}) copy-start(s32[5]{0:T(128)} %stack.23.place) | copy-start | bytes 64
  29.3 4.2 %collective-permute-start.2 = (s32[1,256]{1,0:T(1,128)S(1)}, s32[1,256]{1,0:T(1,128)S(1)}, u32[]{:S(2)}, u32[]{:S(2)}) collective-permute-start(s32[1,256]{1,0:T(1,128)S(1)} %ids_later.1), channel_id=1, source_target_pairs={{0,1},{1,0},{2,3},{3,2},{4,5},{5,4},{6,7},{7,6},{8,9},{9,8},{10,11... | collective-permute-start | bytes 3080 | tf_op jit(solution)/shard_map/ppermute | solution.py:370
  47.2 17.7 %collective-permute-start.5 = (bf16[320,512]{1,0:T(8,128)(2,1)S(1)}, bf16[320,512]{1,0:T(8,128)(2,1)S(1)}, u32[]{:S(2)}, u32[]{:S(2)}) collective-permute-start(bf16[320,512]{1,0:T(8,128)(2,1)S(1)} %strip_ids.1.w0.refs_0_), channel_id=1, source_target_pairs={{0,24},{8,0},{16,8},{24,16},{1,25},{9,1},{17,9},{25,17},{2,26},{10... | collective-permute-start | bytes 983048 | tf_op jit(solution)/shard_map/ppermute | solution.py:366
  51.7 17.9 %collective-permute-start.3 = (bf16[320,512]{1,0:T(8,128)(2,1)S(1)}, bf16[320,512]{1,0:T(8,128)(2,1)S(1)}, u32[]{:S(2)}, u32[]{:S(2)}) collective-permute-start(bf16[320,512]{1,0:T(8,128)(2,1)S(1)} %strip_ids.1.w0.refs_0_), channel_id=1, source_target_pairs={{0,8},{8,16},{16,24},{24,0},{1,9},{9,17},{17,25},{25,1},{2,10},{10... | collective-permute-start | bytes 983048 | tf_op jit(solution)/shard_map/ppermute | solution.py:366
  55.9 15.6 %collective-permute-start.7 = (bf16[192,512]{1,0:T(8,128)(2,1)S(1)}, bf16[192,512]{1,0:T(8,128)(2,1)S(1)}, u32[]{:S(2)}, u32[]{:S(2)}) collective-permute-start(bf16[192,512]{1,0:T(8,128)(2,1)S(1)} %get-tuple-element.23), channel_id=1, source_target_pairs={{0,2},{2,4},{4,6},{6,0},{1,3},{3,5},{5,7},{7,1},{8,10},{10,12},{12... | collective-permute-start | bytes 589832 | tf_op jit(solution)/shard_map/ppermute | solution.py:366
  58.3 13.2 %collective-permute-start.8 = (bf16[192,512]{1,0:T(8,128)(2,1)S(1)}, bf16[192,512]{1,0:T(8,128)(2,1)S(1)}, u32[]{:S(2)}, u32[]{:S(2)}) collective-permute-start(bf16[192,512]{1,0:T(8,128)(2,1)S(1)} %get-tuple-element.24), channel_id=1, source_target_pairs={{0,4},{2,6},{4,0},{6,2},{1,5},{3,7},{5,1},{7,3},{8,12},{10,14},{12... | collective-permute-start | bytes 589832 | tf_op jit(solution)/shard_map/ppermute | solution.py:366
  62.6 8.9 %collective-permute-start.9 = (bf16[192,512]{1,0:T(8,128)(2,1)S(1)}, bf16[192,512]{1,0:T(8,128)(2,1)S(1)}, u32[]{:S(2)}, u32[]{:S(2)}) collective-permute-start(bf16[192,512]{1,0:T(8,128)(2,1)S(1)} %get-tuple-element.25), channel_id=1, source_target_pairs={{0,6},{2,0},{4,2},{6,4},{1,7},{3,1},{5,3},{7,5},{8,14},{10,8},{12,... | collective-permute-start | bytes 589832 | tf_op jit(solution)/shard_map/ppermute | solution.py:366
  64.9 7.6 %collective-permute-start.6 = (bf16[160,512]{1,0:T(8,128)(2,1)S(1)}, bf16[160,512]{1,0:T(8,128)(2,1)S(1)}, u32[]{:S(2)}, u32[]{:S(2)}) collective-permute-start(bf16[160,512]{1,0:T(8,128)(2,1)S(1)} %slice.9), channel_id=1, source_target_pairs={{0,24},{8,0},{16,8},{24,16},{1,25},{9,1},{17,9},{25,17},{2,26},{10... | collective-permute-start | bytes 491528 | tf_op jit(solution)/shard_map/ppermute | solution.py:366
  69.5 8.5 %collective-permute-start.4 = (bf16[160,512]{1,0:T(8,128)(2,1)S(1)}, bf16[160,512]{1,0:T(8,128)(2,1)S(1)}, u32[]{:S(2)}, u32[]{:S(2)}) collective-permute-start(bf16[160,512]{1,0:T(8,128)(2,1)S(1)} %slice.8), channel_id=1, source_target_pairs={{0,8},{8,16},{16,24},{24,0},{1,9},{9,17},{17,25},{25,1},{2,10},{10... | collective-permute-start | bytes 491528 | tf_op jit(solution)/shard_map/ppermute | solution.py:366
  78.0 6.1 %copy-start.2 = (bf16[2,128,512]{2,1,0:T(8,128)(2,1)S(1)}, bf16[2,128,512]{2,1,0:T(8,128)(2,1)}, u32[]{:S(2)}) copy-start(bf16[2,128,512]{2,1,0:T(8,128)(2,1)} %param.8) | copy-start | bytes 786436
  78.1 9.2 %collective-permute-start.10 = (bf16[1664,512]{1,0:T(8,128)(2,1)S(1)}, bf16[1664,512]{1,0:T(8,128)(2,1)S(1)}, u32[]{:S(2)}, u32[]{:S(2)}) collective-permute-start(bf16[1664,512]{1,0:T(8,128)(2,1)S(1)} %pack_for_core.1), channel_id=1, source_target_pairs={{0,1},{1,0},{2,3},{3,2},{4,5},{5,4},{6,7},{7,6},{8,9},{9,8},{10,11... | collective-permute-start | bytes 5111816 | tf_op jit(solution)/shard_map/ppermute | solution.py:370
  87.3 1.8 %copy-start.5 = (s32[2]{0:T(128)S(1)}, s32[2]{0:T(128)}, u32[]{:S(2)}) copy-start(s32[2]{0:T(128)} %lengths.1) | copy-start | bytes 28

commit v4 on v3

--- a/solution.py
+++ b/solution.py
@@ -125,14 +125,16 @@
     before = (iota((count, count), 0) < iota((count, count), 1)).astype(BF16)
     rank = dot(mine.astype(F32).astype(BF16), before)
     key = jnp.where(mine, rank, -1.0)
-    tab = table[...]
     slot = iota((CAP, count), 0).astype(F32)
+    column = iota((CAP, rows), 1).astype(F32)
+    hot = []
     for k in range(8):
         match = slot == key[k : k + 1]
         row_of = jnp.sum(jnp.where(match, local[k : k + 1], 0.0), axis=1, keepdims=True)
-        hot = (iota((CAP, rows), 1).astype(F32) == row_of).astype(BF16)
-        at = (k % 2) * CAP
-        outs[k // 2][at : at + CAP] = dot(hot, tab).astype(BF16)
+        hot.append((column == row_of).astype(BF16))
+    found = dot(jnp.concatenate(hot, axis=0), table[...]).astype(BF16)
+    for k, out in enumerate(outs):
+        out[...] = found[2 * k * CAP : 2 * (k + 1) * CAP]
 
 
 def fetch(place, gathered, table):
@@ -205,11 +207,17 @@
     return rank, offset
 
 
-def place_rows(rank, offset, at, piece):
-    key = jnp.where(offset == at, rank, -1.0)
-    chosen = (iota((CAP, rank.shape[1]), 0).astype(F32) == key).astype(BF16)
+def place_rows(rank, offset, first, pieces):
+    slot = iota((CAP, rank.shape[1]), 0).astype(F32)
+    chosen = [
+        (slot == jnp.where(offset == first + 2 * k, rank, -1.0)).astype(BF16)
+        for k in range(len(pieces))
+    ]
     return lax.dot_general(
-        chosen, piece, (((0,), (0,)), ((), ())), preferred_element_type=F32
+        jnp.concatenate(chosen, axis=0),
+        jnp.concatenate(pieces, axis=0),
+        (((0,), (0,)), ((), ())),
+        preferred_element_type=F32,
     )
 
 
@@ -238,8 +246,7 @@
     for k in range(4):
         part[:, k * width : (k + 1) * width] = dot(normed, weight(k))
     rank, offset = row_keys(place, ids[...])
-    total = place_rows(rank, offset, 0, f0[:CAP]) + place_rows(rank, offset, 2, f1[:CAP])
-    total += place_rows(rank, offset, 4, f2[:CAP]) + place_rows(rank, offset, 6, f3[:CAP])
+    total = place_rows(rank, offset, 0, [f0[:CAP], f1[:CAP], f2[:CAP], f3[:CAP]])
     rows_out[...] = total.astype(BF16)
 
 
@@ -288,10 +295,9 @@
         score = jnp.sum(product[:, cols], axis=-1, keepdims=True) * head ** (-0.5)
         self_term[:, cols] = silu(score).astype(BF16).astype(F32) * value[:, cols]
     rank, offset = row_keys(place, ids[...])
-    total = own_rows[...].astype(F32)
-    for k in range(4):
-        at = other.shape[0] - (4 - k) * CAP
-        total += place_rows(rank, offset, 2 * k + 1, other[at : at + CAP])
+    ends = [other.shape[0] - (4 - k) * CAP for k in range(4)]
+    theirs = place_rows(rank, offset, 1, [other[at : at + CAP] for at in ends])
+    total = own_rows[...].astype(F32) + theirs
     rows_out[...] = total.astype(BF16)
 
 
@@ -322,6 +328,7 @@
     count = cand.shape[0] // users
     lane = iota((1, positions), 1)
     position = (lane % per_owner) * owners + lane // per_owner
+    both = []
     for user in range(users):
         at = slice(user * count, (user + 1) * count)
         length = lengths[user]
@@ -335,18 +342,19 @@
             ) * (head ** (-0.5))
             weights = jnp.where(live, silu(scores), 0.0).astype(BF16)
             parts.append(dot(weights, kv[:, width + h * head : width + (h + 1) * head]))
-        attended = (jnp.concatenate(parts, axis=1) + self_term[at]) * (
-            1.0 / (length.astype(F32) + 1.0)
-        )
-        center = attended - jnp.mean(attended, axis=-1, keepdims=True)
-        spread = jnp.mean(center * center, axis=-1, keepdims=True)
-        gated = (center * lax.rsqrt(spread + 1e-06) * gate[at]).astype(BF16)
-        final = cand[at].astype(F32) + dot(gated, out_weight[...])
-        scale = lax.rsqrt(jnp.mean(final * final, axis=-1, keepdims=True) + 1e-06)
-        unit = (final * scale).astype(BF16).astype(F32)
-        logit = jnp.sum(unit * rows_ref[at].astype(F32), axis=-1, keepdims=True)
-        eye = iota((count, count), 0) == iota((count, count), 1)
-        out[user : user + 1, :] = jnp.sum(jnp.where(eye, logit, 0.0), axis=0, keepdims=True)
+        attended = jnp.concatenate(parts, axis=1) + self_term[at]
+        both.append(attended * (1.0 / (length.astype(F32) + 1.0)))
+    attended = jnp.concatenate(both, axis=0)
+    center = attended - jnp.mean(attended, axis=-1, keepdims=True)
+    spread = jnp.mean(center * center, axis=-1, keepdims=True)
+    gated = (center * gate[...] * lax.rsqrt(spread + 1e-06)).astype(BF16)
+    final = cand[...].astype(F32) + dot(gated, out_weight[...])
+    match = jnp.sum(final * rows_ref[...].astype(F32), axis=-1, keepdims=True)
+    logit = match * lax.rsqrt(jnp.mean(final * final, axis=-1, keepdims=True) + 1e-06)
+    eye = iota((count, count), 0) == iota((count, count), 1)
+    for user in range(users):
+        column = logit[user * count : (user + 1) * count]
+        out[user : user + 1, :] = jnp.sum(jnp.where(eye, column, 0.0), axis=0, keepdims=True)
 
 
 def score(lengths, hist, query, self_term, gate, cand, out_weight, rows):

time: 92.6 us -> 91.5 us (0.988)
  Pallas kernels: 11.7 us -> 10.4 us
  transfers between devices with their start and end apart: 12 -> 12, of which waited for: 4 -> 4; matrix products, arithmetic and copies ran while one was open for 0% -> 0% of each run, Pallas kernels for 7% -> 6%
where the time goes in v4:
time: 91.5 us; the launch traced here: 90.9 us
  starting transfers between devices  57.1 us (62%)
  blocking collectives  13.5 us (15%)
  Pallas kernels  10.4 us (11%)
  waiting for transfers between devices  8.87 us (10%)
    ppermute x7, starting transfers between devices, along(): lax.ppermute(values, axis, [(j, (j + offset) % size) for j in range(size)])  21.8 us
    ppermute x2, starting transfers between devices, body(): lax.ppermute(shard, ('z',) + ITEM, [(k * items + i, (k + i + step) % zs *...  18.6 us
    all_gather x1, blocking collectives, body(): lax.all_gather(block(*shards, my_ids, other_ids), 'x', axis=0, tiled=True)  13.5 us
    ppermute x2, starting transfers between devices, swap_core(): return lax.ppermute(values, 'core', [(0, 1), (1, 0)])  9.23 us
    all_to_all x1, starting transfers between devices, body(): lax.all_to_all(picked, USER, split_axis=0, concat_axis=0, tiled=True)  7.49 us
    ppermute x7, waiting for transfers between devices, along(): lax.ppermute(values, axis, [(j, (j + offset) % size) for j in range(size)])  6.7 us
    pallas_call x1, Pallas kernels, pick(): pl.pallas_call(pick_kernel, out_shape=(jax.ShapeDtypeStruct((rows * 5, wi...  2.53 us
    pallas_call x1, Pallas kernels, score(): pl.pallas_call(score_kernel, out_shape=jax.ShapeDtypeStruct((users, cand....  2.36 us
  transfers between devices with their start and end apart: 12, of which 4 were waited for; matrix products, arithmetic and copies ran while one was open for 0% of the time, Pallas kernels for 6%

profile of v4, /device:TPU:1, one launch (start us, length us, event | category | flops | bytes accessed | tf_op | source)
XLA Modules:
  0.0 90.9 jit_solution(15731446237945304824)
XLA Ops:
  0.0 0.6 stack.23.place
  0.6 2.5 %stack_and_pick.1 = (bf16[40,512]{1,0:T(8,128)(2,1)}, bf16[64,2,4,1024]{3,2,1,0:T(4,128)(2,1)}) custom-call(s32[1024]{0:T(1024)} %slots.1, s32[5]{0:T(128)} %stack.23.place, bf16[8,2048]{1,0:T(8,128)(2,1)} %proj_weight.1, bf16[8,512]{1,0:T(8,128)(2,1)} %out_weight.1, bf16[128,4,1024]{2,1,0:T(4,128)(2,1)} %bitcast.14), custom_call_target="tpu_custom_call" | custom-call | tf_op jit(solution)/shard_map/stack_and_pick/pallas_call | solution.py:85
  3.2 15.9 %collective-permute-start.1 = (bf16[40,512]{1,0:T(8,128)(2,1)}, bf16[40,512]{1,0:T(8,128)(2,1)S(1)}, u32[]{:S(2)}, u32[]{:S(2)}) collective-permute-start(bf16[40,512]{1,0:T(8,128)(2,1)} %get-tuple-element.21), channel_id=1, source_target_pairs={{0,256},{1,289},{2,322},{3,355},{4,388},{5,421},{6,454},{7,487},{3... | collective-permute-start | bytes 122888 | tf_op jit(solution)/shard_map/ppermute | solution.py:397
  19.1 2.6 %collective-permute-start = (bf16[40,512]{1,0:T(8,128)(2,1)}, bf16[40,512]{1,0:T(8,128)(2,1)S(1)}, u32[]{:S(2)}, u32[]{:S(2)}) collective-permute-start(bf16[40,512]{1,0:T(8,128)(2,1)} %get-tuple-element.21), channel_id=1, source_target_pairs={{0,0},{1,33},{2,66},{3,99},{4,132},{5,165},{6,198},{7,231},{32,32}... | collective-permute-start | bytes 122888 | tf_op jit(solution)/shard_map/ppermute | solution.py:397
  21.8 7.5 %all-to-all-start = ((bf16[64,2,4,1024]{3,2,1,0:T(4,128)(2,1)}), bf16[64,2,4,1024]{3,2,1,0:T(4,128)(2,1)S(1)}, u32[]{:S(2)}, u32[]{:S(2)}) async-start(bf16[64,2,4,1024]{3,2,1,0:T(4,128)(2,1)} %get-tuple-element.20.first), calls=%async_computation | async-start | bytes 2097152 | tf_op jit(solution)/shard_map/all_to_all | solution.py:409
  29.3 0.0 copy-start.1
  29.3 3.4 %collective-permute-start.2 = (s32[1,256]{1,0:T(1,128)S(1)}, s32[1,256]{1,0:T(1,128)S(1)}, u32[]{:S(2)}, u32[]{:S(2)}) collective-permute-start(s32[1,256]{1,0:T(1,128)S(1)} %ids_later.1), channel_id=1, source_target_pairs={{0,1},{1,0},{2,3},{3,2},{4,5},{5,4},{6,7},{7,6},{8,9},{9,8},{10,11... | collective-permute-start | bytes 3080 | tf_op jit(solution)/shard_map/ppermute | solution.py:378
  32.7 0.8 collective-permute-done.2.other_ids
  33.5 0.0 collective-permute-done.1.p1
  33.5 0.0 collective-permute-done.p0
  33.5 0.1 block_weights_and_ids.1
  33.7 13.5 %all_gather.3.gathered = bf16[384,512]{1,0:T(8,128)(2,1)S(1)} all-gather(bf16[96,512]{1,0:T(8,128)(2,1)S(1)} %block_weights_and_ids.1), channel_id=1, replica_groups=mesh['z'=16,'y'=4,'x'=4,'core'=2] {'x'}, dimensions={0}, use_global_device_ids=true | all-gather | bytes 491520 | tf_op jit(solution)/shard_map/all_gather | solution.py:414
  47.2 4.4 %collective-permute-start.5 = (bf16[320,512]{1,0:T(8,128)(2,1)S(1)}, bf16[320,512]{1,0:T(8,128)(2,1)S(1)}, u32[]{:S(2)}, u32[]{:S(2)}) collective-permute-start(bf16[320,512]{1,0:T(8,128)(2,1)S(1)} %strip_ids.1.w0.refs_0_), channel_id=1, source_target_pairs={{0,24},{8,0},{16,8},{24,16},{1,25},{9,1},{17,9},{25,17},{2,26},{10... | collective-permute-start | bytes 983048 | tf_op jit(solution)/shard_map/ppermute | solution.py:374
  51.7 1.9 %collective-permute-start.3 = (bf16[320,512]{1,0:T(8,128)(2,1)S(1)}, bf16[320,512]{1,0:T(8,128)(2,1)S(1)}, u32[]{:S(2)}, u32[]{:S(2)}) collective-permute-start(bf16[320,512]{1,0:T(8,128)(2,1)S(1)} %strip_ids.1.w0.refs_0_), channel_id=1, source_target_pairs={{0,8},{8,16},{16,24},{24,0},{1,9},{9,17},{17,25},{25,1},{2,10},{10... | collective-permute-start | bytes 983048 | tf_op jit(solution)/shard_map/ppermute | solution.py:374
  53.6 1.7 %fetch_rows.1 = (bf16[192,512]{1,0:T(8,128)(2,1)S(1)}, bf16[192,512]{1,0:T(8,128)(2,1)S(1)}, bf16[192,512]{1,0:T(8,128)(2,1)S(1)}, bf16[192,512]{1,0:T(8,128)(2,1)S(1)}) custom-call(s32[5]{0:T(128)S(1)} %copy-done.4, bf16[384,512]{1,0:T(8,128)(2,1)S(1)} %all_gather.3.gathered, bf16[1024,512]{1,0:T(8,128)(2,1)S(1)} %copy-done.1), custom_call_target="tpu_custom_call" | custom-call | tf_op jit(solution)/shard_map/fetch_rows/pallas_call | solution.py:141
  55.4 2.4 %collective-permute-start.7 = (bf16[192,512]{1,0:T(8,128)(2,1)S(1)}, bf16[192,512]{1,0:T(8,128)(2,1)S(1)}, u32[]{:S(2)}, u32[]{:S(2)}) collective-permute-start(bf16[192,512]{1,0:T(8,128)(2,1)S(1)} %get-tuple-element.23), channel_id=1, source_target_pairs={{0,2},{2,4},{4,6},{6,0},{1,3},{3,5},{5,7},{7,1},{8,10},{10,12},{12... | collective-permute-start | bytes 589832 | tf_op jit(solution)/shard_map/ppermute | solution.py:374
  57.8 4.3 %collective-permute-start.8 = (bf16[192,512]{1,0:T(8,128)(2,1)S(1)}, bf16[192,512]{1,0:T(8,128)(2,1)S(1)}, u32[]{:S(2)}, u32[]{:S(2)}) collective-permute-start(bf16[192,512]{1,0:T(8,128)(2,1)S(1)} %get-tuple-element.24), channel_id=1, source_target_pairs={{0,4},{2,6},{4,0},{6,2},{1,5},{3,7},{5,1},{7,3},{8,12},{10,14},{12... | collective-permute-start | bytes 589832 | tf_op jit(solution)/shard_map/ppermute | solution.py:374
  62.1 2.3 %collective-permute-start.9 = (bf16[192,512]{1,0:T(8,128)(2,1)S(1)}, bf16[192,512]{1,0:T(8,128)(2,1)S(1)}, u32[]{:S(2)}, u32[]{:S(2)}) collective-permute-start(bf16[192,512]{1,0:T(8,128)(2,1)S(1)} %get-tuple-element.25), channel_id=1, source_target_pairs={{0,6},{2,0},{4,2},{6,4},{1,7},{3,1},{5,3},{7,5},{8,14},{10,8},{12,... | collective-permute-start | bytes 589832 | tf_op jit(solution)/shard_map/ppermute | solution.py:374
  64.4 0.0 collective-permute-done.5.w3.refs_4_
  64.4 4.6 %collective-permute-start.6 = (bf16[160,512]{1,0:T(8,128)(2,1)S(1)}, bf16[160,512]{1,0:T(8,128)(2,1)S(1)}, u32[]{:S(2)}, u32[]{:S(2)}) collective-permute-start(bf16[160,512]{1,0:T(8,128)(2,1)S(1)} %slice.9), channel_id=1, source_target_pairs={{0,24},{8,0},{16,8},{24,16},{1,25},{9,1},{17,9},{25,17},{2,26},{10... | collective-permute-start | bytes 491528 | tf_op jit(solution)/shard_map/ppermute | solution.py:374
  69.0 0.0 collective-permute-done.3.w1.refs_1_
  69.0 1.9 %collective-permute-start.4 = (bf16[160,512]{1,0:T(8,128)(2,1)S(1)}, bf16[160,512]{1,0:T(8,128)(2,1)S(1)}, u32[]{:S(2)}, u32[]{:S(2)}) collective-permute-start(bf16[160,512]{1,0:T(8,128)(2,1)S(1)} %slice.8), channel_id=1, source_target_pairs={{0,8},{8,16},{16,24},{24,0},{1,9},{9,17},{17,25},{25,1},{2,10},{10... | collective-permute-start | bytes 491528 | tf_op jit(solution)/shard_map/ppermute | solution.py:374
  70.9 0.0 collective-permute-done.8.f2.refs_7_
  71.0 0.9 collective-permute-done.6.w2b.refs_3_
  71.8 5.8 %collective-permute-done.4.w2a.refs_2_ = bf16[160,512]{1,0:T(8,128)(2,1)S(1)} collective-permute-done((bf16[160,512]{1,0:T(8,128)(2,1)S(1)}, bf16[160,512]{1,0:T(8,128)(2,1)S(1)}, u32[]{:S(2)}, u32[]{:S(2)}) %collective-permute-start.4) | collective-permute-done | bytes 163872 | tf_op jit(solution)/shard_map/ppermute | solution.py:374
  77.7 0.1 pack_for_core.1
  77.8 5.8 %collective-permute-start.10 = (bf16[1664,512]{1,0:T(8,128)(2,1)S(1)}, bf16[1664,512]{1,0:T(8,128)(2,1)S(1)}, u32[]{:S(2)}, u32[]{:S(2)}) collective-permute-start(bf16[1664,512]{1,0:T(8,128)(2,1)S(1)} %pack_for_core.1), channel_id=1, source_target_pairs={{0,1},{1,0},{2,3},{3,2},{4,5},{5,4},{6,7},{7,6},{8,9},{9,8},{10,11... | collective-permute-start | bytes 5111816 | tf_op jit(solution)/shard_map/ppermute | solution.py:378
  83.6 1.8 %project_own.1 = (f32[256,2048]{1,0:T(8,128)S(1)}, bf16[256,256]{1,0:T(8,128)(2,1)S(1)}, bf16[512,512]{1,0:T(8,128)(2,1)S(1)}, bf16[256,512]{1,0:T(8,128)(2,1)S(1)}) custom-call(s32[5]{0:T(128)S(1)} %copy-done.4, s32[1,256]{1,0:T(1,128)S(1)} %bitcast.12, bf16[256,512]{1,0:T(8,128)(2,1)S(1)} %bitcast.8, bf16[320,512]{1,0:T(8,128)(2,1)S(1)} %strip_ids.1.w0.refs_0_, ...), custom_call_target="tpu_custom_call" | custom-call | tf_op jit(solution)/shard_map/project_own/pallas_call | solution.py:255
  85.5 1.4 %collective-permute-done.10.other = bf16[1664,512]{1,0:T(8,128)(2,1)S(1)} collective-permute-done((bf16[1664,512]{1,0:T(8,128)(2,1)S(1)}, bf16[1664,512]{1,0:T(8,128)(2,1)S(1)}, u32[]{:S(2)}, u32[]{:S(2)}) %collective-permute-start.10) | collective-permute-done | bytes 1703968 | tf_op jit(solution)/shard_map/ppermute | solution.py:378
  86.8 1.7 %project.1 = (f32[256,512]{1,0:T(8,128)S(1)}, bf16[256,512]{1,0:T(8,128)(2,1)S(1)}, f32[256,512]{1,0:T(8,128)S(1)}, bf16[512,512]{1,0:T(8,128)(2,1)S(1)}, bf16[256,512]{1,0:T(8,128)(2,1)S(1)}) custom-call(s32[5]{0:T(128)S(1)} %copy-done.4, s32[1,256]{1,0:T(1,128)S(1)} %bitcast.13, f32[256,2048]{1,0:T(8,128)S(1)} %get-tuple-element.26.part, ...), custom_call_target="tpu_custom_call" | custom-call | flops 19000000512 | tf_op jit(solution)/shard_map/project/pallas_call | solution.py:306
  88.5 0.0 all-to-all-done.hist
  88.5 2.4 %score.1 = f32[2,128]{1,0:T(2,128)} custom-call(s32[2]{0:T(128)S(1)} %copy-done.5, bf16[64,2,4,1024]{3,2,1,0:T(4,128)(2,1)S(1)} %all-to-all-done.hist, bf16[256,512]{1,0:T(8,128)(2,1)S(1)} %get-tuple-element.30.query, f32[256,512]{1,0:T(8,128)S(1)} %get-tuple-element.31.self_term, f32[256,512]{1,0:T(8,128)S(1)} %get-tuple-element.32.gate, ...), custom_call_target="tpu_custom_call" | custom-call | tf_op jit(solution)/shard_map/score/pallas_call | solution.py:362
  (17 shorter events, 0.1 us)
Async XLA Ops:
  0.0 29.3 %copy-start.3 = (s32[2,128]{1,0:T(2,128)S(1)}, s32[2,128]{1,0:T(2,128)}, u32[]{:S(2)}) copy-start(s32[2,128]{1,0:T(2,128)} %param.14) | copy-start | bytes 3076
  3.1 26.1 %copy-start = (bf16[64,2,4,1024]{3,2,1,0:T(4,128)(2,1)S(1)}, bf16[64,2,4,1024]{3,2,1,0:T(4,128)(2,1)}, u32[]{:S(2)}) copy-start(bf16[64,2,4,1024]{3,2,1,0:T(4,128)(2,1)} %get-tuple-element.20.first) | copy-start | bytes 3145732
  3.2 30.4 %collective-permute-start.1 = (bf16[40,512]{1,0:T(8,128)(2,1)}, bf16[40,512]{1,0:T(8,128)(2,1)S(1)}, u32[]{:S(2)}, u32[]{:S(2)}) collective-permute-start(bf16[40,512]{1,0:T(8,128)(2,1)} %get-tuple-element.21), channel_id=1, source_target_pairs={{0,256},{1,289},{2,322},{3,355},{4,388},{5,421},{6,454},{7,487},{3... | collective-permute-start | bytes 122888 | tf_op jit(solution)/shard_map/ppermute | solution.py:397
  19.1 14.4 %collective-permute-start = (bf16[40,512]{1,0:T(8,128)(2,1)}, bf16[40,512]{1,0:T(8,128)(2,1)S(1)}, u32[]{:S(2)}, u32[]{:S(2)}) collective-permute-start(bf16[40,512]{1,0:T(8,128)(2,1)} %get-tuple-element.21), channel_id=1, source_target_pairs={{0,0},{1,33},{2,66},{3,99},{4,132},{5,165},{6,198},{7,231},{32,32}... | collective-permute-start | bytes 122888 | tf_op jit(solution)/shard_map/ppermute | solution.py:397
  21.8 66.8 %all-to-all-start = ((bf16[64,2,4,1024]{3,2,1,0:T(4,128)(2,1)}), bf16[64,2,4,1024]{3,2,1,0:T(4,128)(2,1)S(1)}, u32[]{:S(2)}, u32[]{:S(2)}) async-start(bf16[64,2,4,1024]{3,2,1,0:T(4,128)(2,1)} %get-tuple-element.20.first), calls=%async_computation | async-start | bytes 2097152 | tf_op jit(solution)/shard_map/all_to_all | solution.py:409
  29.3 24.3 %copy-start.1 = (bf16[1024,512]{1,0:T(8,128)(2,1)S(1)}, bf16[1024,512]{1,0:T(8,128)(2,1)}, u32[]{:S(2)}) copy-start(bf16[1024,512]{1,0:T(8,128)(2,1)} %table.1) | copy-start | bytes 3145732
  29.3 24.3 %copy-start.4 = (s32[5]{0:T(128)S(1)}, s32[5]{0:T(128)}, u32[]{:S(2)}) copy-start(s32[5]{0:T(128)} %stack.23.place) | copy-start | bytes 64
  29.3 4.2 %collective-permute-start.2 = (s32[1,256]{1,0:T(1,128)S(1)}, s32[1,256]{1,0:T(1,128)S(1)}, u32[]{:S(2)}, u32[]{:S(2)}) collective-permute-start(s32[1,256]{1,0:T(1,128)S(1)} %ids_later.1), channel_id=1, source_target_pairs={{0,1},{1,0},{2,3},{3,2},{4,5},{5,4},{6,7},{7,6},{8,9},{9,8},{10,11... | collective-permute-start | bytes 3080 | tf_op jit(solution)/shard_map/ppermute | solution.py:378
  47.2 17.1 %collective-permute-start.5 = (bf16[320,512]{1,0:T(8,128)(2,1)S(1)}, bf16[320,512]{1,0:T(8,128)(2,1)S(1)}, u32[]{:S(2)}, u32[]{:S(2)}) collective-permute-start(bf16[320,512]{1,0:T(8,128)(2,1)S(1)} %strip_ids.1.w0.refs_0_), channel_id=1, source_target_pairs={{0,24},{8,0},{16,8},{24,16},{1,25},{9,1},{17,9},{25,17},{2,26},{10... | collective-permute-start | bytes 983048 | tf_op jit(solution)/shard_map/ppermute | solution.py:374
  51.7 17.3 %collective-permute-start.3 = (bf16[320,512]{1,0:T(8,128)(2,1)S(1)}, bf16[320,512]{1,0:T(8,128)(2,1)S(1)}, u32[]{:S(2)}, u32[]{:S(2)}) collective-permute-start(bf16[320,512]{1,0:T(8,128)(2,1)S(1)} %strip_ids.1.w0.refs_0_), channel_id=1, source_target_pairs={{0,8},{8,16},{16,24},{24,0},{1,9},{9,17},{17,25},{25,1},{2,10},{10... | collective-permute-start | bytes 983048 | tf_op jit(solution)/shard_map/ppermute | solution.py:374
  55.4 15.6 %collective-permute-start.7 = (bf16[192,512]{1,0:T(8,128)(2,1)S(1)}, bf16[192,512]{1,0:T(8,128)(2,1)S(1)}, u32[]{:S(2)}, u32[]{:S(2)}) collective-permute-start(bf16[192,512]{1,0:T(8,128)(2,1)S(1)} %get-tuple-element.23), channel_id=1, source_target_pairs={{0,2},{2,4},{4,6},{6,0},{1,3},{3,5},{5,7},{7,1},{8,10},{10,12},{12... | collective-permute-start | bytes 589832 | tf_op jit(solution)/shard_map/ppermute | solution.py:374
  57.8 13.2 %collective-permute-start.8 = (bf16[192,512]{1,0:T(8,128)(2,1)S(1)}, bf16[192,512]{1,0:T(8,128)(2,1)S(1)}, u32[]{:S(2)}, u32[]{:S(2)}) collective-permute-start(bf16[192,512]{1,0:T(8,128)(2,1)S(1)} %get-tuple-element.24), channel_id=1, source_target_pairs={{0,4},{2,6},{4,0},{6,2},{1,5},{3,7},{5,1},{7,3},{8,12},{10,14},{12... | collective-permute-start | bytes 589832 | tf_op jit(solution)/shard_map/ppermute | solution.py:374
  62.1 8.9 %collective-permute-start.9 = (bf16[192,512]{1,0:T(8,128)(2,1)S(1)}, bf16[192,512]{1,0:T(8,128)(2,1)S(1)}, u32[]{:S(2)}, u32[]{:S(2)}) collective-permute-start(bf16[192,512]{1,0:T(8,128)(2,1)S(1)} %get-tuple-element.25), channel_id=1, source_target_pairs={{0,6},{2,0},{4,2},{6,4},{1,7},{3,1},{5,3},{7,5},{8,14},{10,8},{12,... | collective-permute-start | bytes 589832 | tf_op jit(solution)/shard_map/ppermute | solution.py:374
  64.4 7.4 %collective-permute-start.6 = (bf16[160,512]{1,0:T(8,128)(2,1)S(1)}, bf16[160,512]{1,0:T(8,128)(2,1)S(1)}, u32[]{:S(2)}, u32[]{:S(2)}) collective-permute-start(bf16[160,512]{1,0:T(8,128)(2,1)S(1)} %slice.9), channel_id=1, source_target_pairs={{0,24},{8,0},{16,8},{24,16},{1,25},{9,1},{17,9},{25,17},{2,26},{10... | collective-permute-start | bytes 491528 | tf_op jit(solution)/shard_map/ppermute | solution.py:374
  69.0 8.6 %collective-permute-start.4 = (bf16[160,512]{1,0:T(8,128)(2,1)S(1)}, bf16[160,512]{1,0:T(8,128)(2,1)S(1)}, u32[]{:S(2)}, u32[]{:S(2)}) collective-permute-start(bf16[160,512]{1,0:T(8,128)(2,1)S(1)} %slice.8), channel_id=1, source_target_pairs={{0,8},{8,16},{16,24},{24,0},{1,9},{9,17},{17,25},{25,1},{2,10},{10... | collective-permute-start | bytes 491528 | tf_op jit(solution)/shard_map/ppermute | solution.py:374
  77.7 6.0 %copy-start.2 = (bf16[2,128,512]{2,1,0:T(8,128)(2,1)S(1)}, bf16[2,128,512]{2,1,0:T(8,128)(2,1)}, u32[]{:S(2)}) copy-start(bf16[2,128,512]{2,1,0:T(8,128)(2,1)} %param.8) | copy-start | bytes 786436
  77.8 9.0 %collective-permute-start.10 = (bf16[1664,512]{1,0:T(8,128)(2,1)S(1)}, bf16[1664,512]{1,0:T(8,128)(2,1)S(1)}, u32[]{:S(2)}, u32[]{:S(2)}) collective-permute-start(bf16[1664,512]{1,0:T(8,128)(2,1)S(1)} %pack_for_core.1), channel_id=1, source_target_pairs={{0,1},{1,0},{2,3},{3,2},{4,5},{5,4},{6,7},{7,6},{8,9},{9,8},{10,11... | collective-permute-start | bytes 5111816 | tf_op jit(solution)/shard_map/ppermute | solution.py:378
  86.8 1.7 %copy-start.5 = (s32[2]{0:T(128)S(1)}, s32[2]{0:T(128)}, u32[]{:S(2)}) copy-start(s32[2]{0:T(128)} %lengths.1) | copy-start | bytes 28

commit v5 on v4

--- a/solution.py
+++ b/solution.py
@@ -37,28 +37,27 @@
     return jnp.dot(a, b, preferred_element_type=F32)
 
 
-def block_kernel(p0, p1, my_ids, other_ids, out):
+def block_kernel(p0, p1, ids, out):
     rows = jnp.concatenate([p0[...].astype(F32), p1[...].astype(F32)], axis=0).astype(BF16)
     count = rows.shape[0]
     k = iota((count, count), 0)
     source = (k % 16) // 8 * (count // 2) + k // 16 * 8 + k % 8
     move = (iota((count, count), 1) == source).astype(BF16)
-    ids = jnp.concatenate([my_ids[...], other_ids[...]], axis=0)
-    digits = jnp.concatenate([ids // 128, ids % 128], axis=1).astype(F32)
-    rest = jnp.zeros((out.shape[0] - count - 2, out.shape[1]), F32)
+    digits = jnp.concatenate([ids[...] // 128, ids[...] % 128], axis=1).astype(F32)
+    rest = jnp.zeros((out.shape[0] - count - 1, out.shape[1]), F32)
     out[...] = jnp.concatenate([dot(move, rows), digits, rest], axis=0).astype(BF16)
 
 
-def block(p0, p1, my_ids, other_ids):
+def block(p0, p1, ids):
     rows, width = p0.shape
     return pl.pallas_call(
         block_kernel,
         out_shape=jax.ShapeDtypeStruct((2 * rows + 16, width), BF16),
-        in_specs=[pl.BlockSpec(memory_space=VMEM)] * 4,
+        in_specs=[pl.BlockSpec(memory_space=VMEM)] * 3,
         out_specs=pl.BlockSpec(memory_space=VMEM),
         compiler_params=params(),
         name="block_weights_and_ids",
-    )(p0, p1, my_ids, other_ids)
+    )(p0, p1, ids)
 
 
 def pick_kernel(slots, place, proj_weight, out_weight, hist, shard, out):
@@ -106,85 +105,88 @@
         in_specs=[pl.BlockSpec(memory_space=pl.ANY), pl.BlockSpec(memory_space=VMEM)],
         out_specs=pl.BlockSpec(memory_space=VMEM),
         compiler_params=params(),
-        name="ids_later",
+        name="table_later",
     )(first, values)
 
 
-def fetch_kernel(place, gathered, table, *outs):
-    item, x = place[0], place[1]
+def fetch_kernel(place, gathered, table, other_table, *outs):
+    x, core = place[1], place[2]
     rows = table.shape[0]
     step = gathered.shape[0] // 4
     parts = []
     for k in range(4):
         at = pl.multiple_of((x + k) % 4 * step + step - 16, 16)
-        parts.append(gathered[pl.ds(at, 16), :].astype(F32)[:2])
+        parts.append(gathered[pl.ds(at, 16), :].astype(F32)[:1])
     digits = jnp.concatenate(parts, axis=0)
     count = digits.shape[1] // 2
-    local = digits[:, :count] * 128.0 + digits[:, count:] - (item * rows).astype(F32)
-    mine = (local >= 0.0) & (local < float(rows))
+    ids = digits[:, :count] * 128.0 + digits[:, count:]
     before = (iota((count, count), 0) < iota((count, count), 1)).astype(BF16)
-    rank = dot(mine.astype(F32).astype(BF16), before)
-    key = jnp.where(mine, rank, -1.0)
     slot = iota((CAP, count), 0).astype(F32)
     column = iota((CAP, rows), 1).astype(F32)
-    hot = []
-    for k in range(8):
-        match = slot == key[k : k + 1]
-        row_of = jnp.sum(jnp.where(match, local[k : k + 1], 0.0), axis=1, keepdims=True)
-        hot.append((column == row_of).astype(BF16))
-    found = dot(jnp.concatenate(hot, axis=0), table[...]).astype(BF16)
-    for k, out in enumerate(outs):
-        out[...] = found[2 * k * CAP : 2 * (k + 1) * CAP]
-
-
-def fetch(place, gathered, table):
+    for side, tab in enumerate((table, other_table)):
+        local = ids - ((x * 2 + (core + side) % 2) * rows).astype(F32)
+        mine = (local >= 0.0) & (local < float(rows))
+        rank = dot(mine.astype(F32).astype(BF16), before)
+        key = jnp.where(mine, rank, -1.0)
+        hot = []
+        for k in range(4):
+            match = slot == key[k : k + 1]
+            row_of = jnp.sum(jnp.where(match, local[k : k + 1], 0.0), axis=1, keepdims=True)
+            hot.append((column == row_of).astype(BF16))
+        found = dot(jnp.concatenate(hot, axis=0), tab[...]).astype(BF16)
+        for k, out in enumerate(outs):
+            out[side * CAP : (side + 1) * CAP] = found[k * CAP : (k + 1) * CAP]
+
+
+def fetch(place, gathered, table, other_table):
     return pl.pallas_call(
         fetch_kernel,
         out_shape=(jax.ShapeDtypeStruct((2 * CAP, table.shape[1]), table.dtype),) * 4,
-        in_specs=[pl.BlockSpec(memory_space=SMEM)] + [pl.BlockSpec(memory_space=VMEM)] * 2,
+        in_specs=[pl.BlockSpec(memory_space=SMEM)] + [pl.BlockSpec(memory_space=VMEM)] * 3,
         out_specs=(pl.BlockSpec(memory_space=VMEM),) * 4,
         compiler_params=params(),
         name="fetch_rows",
-    )(place, gathered, table)
-
-
-def strip_kernel(gathered, out):
+    )(place, gathered, table, other_table)
+
+
+def strip_kernel(gathered, first, out):
     step, keep = gathered.shape[0] // 4, out.shape[0] // 4
     for k in range(4):
         out[k * keep : (k + 1) * keep] = gathered[k * step : k * step + keep]
 
 
-def strip(gathered):
+def strip(gathered, first):
     rows, width = gathered.shape
     return pl.pallas_call(
         strip_kernel,
         out_shape=jax.ShapeDtypeStruct((rows - 64, width), BF16),
-        in_specs=[pl.BlockSpec(memory_space=VMEM)],
+        in_specs=[pl.BlockSpec(memory_space=VMEM), pl.BlockSpec(memory_space=pl.ANY)],
         out_specs=pl.BlockSpec(memory_space=VMEM),
         compiler_params=params(),
         name="strip_ids",
-    )(gathered)
+    )(gathered, first)
 
 
 def pack_kernel(starts, *refs):
     out = refs[-1]
     at = 0
-    for start, ref in zip(starts, refs[:-1]):
+    for start, ref in zip(starts, refs):
         rows = ref.shape[0] - start
         out[at : at + rows] = ref[start:]
         at += rows
 
 
-def pack(starts, pieces):
+def pack(starts, pieces, first):
     rows = sum(piece.shape[0] - start for start, piece in zip(starts, pieces))
     return pl.pallas_call(
         functools.partial(pack_kernel, starts),
         out_shape=jax.ShapeDtypeStruct((rows, pieces[0].shape[1]), BF16),
-        in_specs=[pl.BlockSpec(memory_space=VMEM)] * len(pieces),
+        in_specs=[pl.BlockSpec(memory_space=VMEM)] * len(pieces)
+        + [pl.BlockSpec(memory_space=pl.ANY)] * len(first),
         out_specs=pl.BlockSpec(memory_space=VMEM),
         compiler_params=params(),
         name="pack_for_core",
-    )(*pieces)
+    )(*pieces, *first)
 
 
 def natural_rows(place, half, size):
@@ -247,6 +249,7 @@
         part[:, k * width : (k + 1) * width] = dot(normed, weight(k))
     rank, offset = row_keys(place, ids[...])
     total = place_rows(rank, offset, 0, [f0[:CAP], f1[:CAP], f2[:CAP], f3[:CAP]])
+    total += place_rows(rank, offset, 1, [f0[CAP:], f1[CAP:], f2[CAP:], f3[CAP:]])
     rows_out[...] = total.astype(BF16)
 
 
@@ -267,11 +270,9 @@
     )(place, ids, cand, *pieces, *found)
 
 
-def rest_kernel(
-    place, ids, part, rest, own_weight, own_rows, other, gate, query, self_term, out_weight, rows_out
-):
-    width = own_rows.shape[1]
-    shard = (other.shape[0] - 4 * CAP) // 4
+def rest_kernel(place, part, rest, own_weight, other, gate, query, self_term, out_weight):
+    width = own_weight.shape[1]
+    shard = other.shape[0] // 4
     normed = rest[...]
 
     def weight(cols):
@@ -294,15 +295,10 @@
         cols = slice(h * head, (h + 1) * head)
         score = jnp.sum(product[:, cols], axis=-1, keepdims=True) * head ** (-0.5)
         self_term[:, cols] = silu(score).astype(BF16).astype(F32) * value[:, cols]
-    rank, offset = row_keys(place, ids[...])
-    ends = [other.shape[0] - (4 - k) * CAP for k in range(4)]
-    theirs = place_rows(rank, offset, 1, [other[at : at + CAP] for at in ends])
-    total = own_rows[...].astype(F32) + theirs
-    rows_out[...] = total.astype(BF16)
-
-
-def project_rest(place, ids, own, other):
-    rows, width = own[3].shape
+
+
+def project_rest(place, part, rest, own_weight, other):
+    rows, width = part.shape[0], own_weight.shape[1]
     return pl.pallas_call(
         rest_kernel,
         out_shape=(
@@ -310,14 +306,13 @@
             jax.ShapeDtypeStruct((rows, width), BF16),
             jax.ShapeDtypeStruct((rows, width), F32),
             jax.ShapeDtypeStruct((width, width), BF16),
-            jax.ShapeDtypeStruct((rows, width), BF16),
         ),
-        in_specs=[pl.BlockSpec(memory_space=SMEM)] + [pl.BlockSpec(memory_space=VMEM)] * 6,
-        out_specs=(pl.BlockSpec(memory_space=VMEM),) * 5,
+        in_specs=[pl.BlockSpec(memory_space=SMEM)] + [pl.BlockSpec(memory_space=VMEM)] * 4,
+        out_specs=(pl.BlockSpec(memory_space=VMEM),) * 4,
         compiler_params=params(),
         name="project",
-        cost_estimate=pl.CostEstimate(flops=int(1.9e10), bytes_accessed=0, transcendentals=0),
-    )(place, ids, *own, other)
+        cost_estimate=pl.CostEstimate(flops=int(1.34e10), bytes_accessed=0, transcendentals=0),
+    )(place, part, rest, own_weight, other)
 
 
 def score_kernel(lengths, hist, query, self_term, gate, cand, out_weight, rows_ref, out):
@@ -409,21 +404,22 @@
     arrived = lax.all_to_all(picked, USER, split_axis=0, concat_axis=0, tiled=True)
 
     my_ids = cand_item.reshape(1, users * count)
-    other_ids = swap_core(later(picked, my_ids))
-
-    gathered = lax.all_gather(block(*shards, my_ids, other_ids), "x", axis=0, tiled=True)
-    weight = strip(gathered)
+
+    blocked = block(*shards, my_ids)
+    gathered = lax.all_gather(blocked, "x", axis=0, tiled=True)
+    other_table = swap_core(later(blocked, item_table))
+    weight = strip(gathered, other_table)
     half = weight.shape[0] // 2
     left, right = along("y", weight, 1), along("y", weight, 3)
     far_top, far_end = along("y", left[:half], 1), along("y", right[half:], 3)
     pieces = [weight, left, far_top, far_end, right]
 
-    found = list(fetch(place, gathered, item_table))
+    found = list(fetch(place, gathered, item_table, other_table))
     for k in (1, 3, 2):
         found[k] = along("x", found[k], k)
-    other = swap_core(pack((0,) * 5 + (CAP,) * 4, pieces + found))
-    own = project_own(place, my_ids, cand, pieces, found)
-    gate, query, self_term, out_w, rows = project_rest(place, my_ids, own, other)
+    other = swap_core(pack((0,) * 5, pieces, found[1:]))
+    part, rest, own_weight, rows = project_own(place, my_ids, cand, pieces, found)
+    gate, query, self_term, out_w = project_rest(place, part, rest, own_weight, other)
     return score(hist_len, arrived, query, self_term, gate, cand, out_w, rows)
 
 

time: 91.5 us -> 89.5 us (0.978)
  the two profiles are of different devices: /device:TPU:1 before, /device:TPU:6 now
where the time goes in v5:
time: 89.5 us; the launch traced here: 89 us
  starting transfers between devices  55.3 us (62%)
  blocking collectives  12.6 us (14%)
  Pallas kernels  10.7 us (12%)
  waiting for transfers between devices  9.4 us (11%)
    ppermute x7, starting transfers between devices, along(): lax.ppermute(values, axis, [(j, (j + offset) % size) for j in range(size)])  22.8 us
    ppermute x2, starting transfers between devices, body(): lax.ppermute(shard, ('z',) + ITEM, [(k * items + i, (k + i + step) % zs *...  14.7 us
    all_to_all x1, starting transfers between devices, body(): lax.all_to_all(picked, USER, split_axis=0, concat_axis=0, tiled=True)  13.9 us
    all_gather x1, blocking collectives, body(): gathered = lax.all_gather(blocked, 'x', axis=0, tiled=True)  12.6 us
    all_to_all x1, waiting for transfers between devices, body(): lax.all_to_all(picked, USER, split_axis=0, concat_axis=0, tiled=True)  5.03 us
    ppermute x2, starting transfers between devices, swap_core(): return lax.ppermute(values, 'core', [(0, 1), (1, 0)])  3.84 us
    ppermute x7, waiting for transfers between devices, along(): lax.ppermute(values, axis, [(j, (j + offset) % size) for j in range(size)])  3.34 us
    pallas_call x1, Pallas kernels, pick(): pl.pallas_call(pick_kernel, out_shape=(jax.ShapeDtypeStruct((rows * 5, wi...  2.52 us
  transfers between devices with their start and end apart: 12, of which 4 were waited for; matrix products, arithmetic and copies ran while one was open for 0% of the time, Pallas kernels for 7%

profile of v5, /device:TPU:6, one launch (start us, length us, event | category | flops | bytes accessed | tf_op | source)
XLA Modules:
  0.0 89.0 jit_solution(264542427711290715)
XLA Ops:
  0.0 0.7 stack.23.place
  0.7 2.5 %stack_and_pick.1 = (bf16[40,512]{1,0:T(8,128)(2,1)}, bf16[64,2,4,1024]{3,2,1,0:T(4,128)(2,1)}) custom-call(s32[1024]{0:T(1024)} %slots.1, s32[5]{0:T(128)} %stack.23.place, bf16[8,2048]{1,0:T(8,128)(2,1)} %proj_weight.1, bf16[8,512]{1,0:T(8,128)(2,1)} %out_weight.1, bf16[128,4,1024]{2,1,0:T(4,128)(2,1)} %bitcast.12), custom_call_target="tpu_custom_call" | custom-call | tf_op jit(solution)/shard_map/stack_and_pick/pallas_call | solution.py:84
  3.2 11.9 %collective-permute-start = (bf16[40,512]{1,0:T(8,128)(2,1)}, bf16[40,512]{1,0:T(8,128)(2,1)S(1)}, u32[]{:S(2)}, u32[]{:S(2)}) collective-permute-start(bf16[40,512]{1,0:T(8,128)(2,1)} %get-tuple-element.20), channel_id=1, source_target_pairs={{0,0},{1,33},{2,66},{3,99},{4,132},{5,165},{6,198},{7,231},{32,32}... | collective-permute-start | bytes 122888 | tf_op jit(solution)/shard_map/ppermute | solution.py:392
  15.1 2.8 %collective-permute-start.1 = (bf16[40,512]{1,0:T(8,128)(2,1)}, bf16[40,512]{1,0:T(8,128)(2,1)S(1)}, u32[]{:S(2)}, u32[]{:S(2)}) collective-permute-start(bf16[40,512]{1,0:T(8,128)(2,1)} %get-tuple-element.20), channel_id=1, source_target_pairs={{0,256},{1,289},{2,322},{3,355},{4,388},{5,421},{6,454},{7,487},{3... | collective-permute-start | bytes 122888 | tf_op jit(solution)/shard_map/ppermute | solution.py:392
  17.9 13.9 %all-to-all-start = ((bf16[64,2,4,1024]{3,2,1,0:T(4,128)(2,1)}), bf16[64,2,4,1024]{3,2,1,0:T(4,128)(2,1)S(1)}, u32[]{:S(2)}, u32[]{:S(2)}) async-start(bf16[64,2,4,1024]{3,2,1,0:T(4,128)(2,1)} %get-tuple-element.19), calls=%async_computation | async-start | bytes 2097152 | tf_op jit(solution)/shard_map/all_to_all | solution.py:404
  31.8 0.0 collective-permute-done.p0
  31.9 0.0 collective-permute-done.1.p1
  31.9 0.1 block_weights_and_ids.1.first
  32.0 0.1 table_later.1
  32.1 1.9 %collective-permute-start.2 = (bf16[1024,512]{1,0:T(8,128)(2,1)S(1)}, bf16[1024,512]{1,0:T(8,128)(2,1)S(1)}, u32[]{:S(2)}, u32[]{:S(2)}) collective-permute-start(bf16[1024,512]{1,0:T(8,128)(2,1)S(1)} %table_later.1), channel_id=1, source_target_pairs={{0,1},{1,0},{2,3},{3,2},{4,5},{5,4},{6,7},{7,6},{8,9},{9,8},{10,11... | collective-permute-start | bytes 3145736 | tf_op jit(solution)/shard_map/ppermute | solution.py:373
  34.0 12.6 %all_gather.3.gathered = bf16[384,512]{1,0:T(8,128)(2,1)S(1)} all-gather(bf16[96,512]{1,0:T(8,128)(2,1)S(1)} %block_weights_and_ids.1.first), channel_id=1, replica_groups=mesh['z'=16,'y'=4,'x'=4,'core'=2] {'x'}, dimensions={0}, use_global_device_ids=true | all-gather | bytes 491520 | tf_op jit(solution)/shard_map/all_gather | solution.py:409
  46.7 3.5 %collective-permute-start.3 = (bf16[320,512]{1,0:T(8,128)(2,1)S(1)}, bf16[320,512]{1,0:T(8,128)(2,1)S(1)}, u32[]{:S(2)}, u32[]{:S(2)}) collective-permute-start(bf16[320,512]{1,0:T(8,128)(2,1)S(1)} %strip_ids.1.w0.refs_0_), channel_id=1, source_target_pairs={{0,8},{8,16},{16,24},{24,0},{1,9},{9,17},{17,25},{25,1},{2,10},{10... | collective-permute-start | bytes 983048 | tf_op jit(solution)/shard_map/ppermute | solution.py:369
  50.1 3.6 %collective-permute-start.5 = (bf16[320,512]{1,0:T(8,128)(2,1)S(1)}, bf16[320,512]{1,0:T(8,128)(2,1)S(1)}, u32[]{:S(2)}, u32[]{:S(2)}) collective-permute-start(bf16[320,512]{1,0:T(8,128)(2,1)S(1)} %strip_ids.1.w0.refs_0_), channel_id=1, source_target_pairs={{0,24},{8,0},{16,8},{24,16},{1,25},{9,1},{17,9},{25,17},{2,26},{10... | collective-permute-start | bytes 983048 | tf_op jit(solution)/shard_map/ppermute | solution.py:369
  53.7 2.0 %fetch_rows.1 = (bf16[192,512]{1,0:T(8,128)(2,1)S(1)}, bf16[192,512]{1,0:T(8,128)(2,1)S(1)}, bf16[192,512]{1,0:T(8,128)(2,1)S(1)}, bf16[192,512]{1,0:T(8,128)(2,1)S(1)}) custom-call(s32[5]{0:T(128)S(1)} %copy-done.2, bf16[384,512]{1,0:T(8,128)(2,1)S(1)} %all_gather.3.gathered, bf16[1024,512]{1,0:T(8,128)(2,1)S(1)} %copy-done, ...), custom_call_target="tpu_custom_call" | custom-call | tf_op jit(solution)/shard_map/fetch_rows/pallas_call | solution.py:142
  55.7 2.7 %collective-permute-start.7 = (bf16[192,512]{1,0:T(8,128)(2,1)S(1)}, bf16[192,512]{1,0:T(8,128)(2,1)S(1)}, u32[]{:S(2)}, u32[]{:S(2)}) collective-permute-start(bf16[192,512]{1,0:T(8,128)(2,1)S(1)} %get-tuple-element.22), channel_id=1, source_target_pairs={{0,2},{2,4},{4,6},{6,0},{1,3},{3,5},{5,7},{7,1},{8,10},{10,12},{12... | collective-permute-start | bytes 589832 | tf_op jit(solution)/shard_map/ppermute | solution.py:369
  58.4 2.8 %collective-permute-start.8 = (bf16[192,512]{1,0:T(8,128)(2,1)S(1)}, bf16[192,512]{1,0:T(8,128)(2,1)S(1)}, u32[]{:S(2)}, u32[]{:S(2)}) collective-permute-start(bf16[192,512]{1,0:T(8,128)(2,1)S(1)} %get-tuple-element.23), channel_id=1, source_target_pairs={{0,4},{2,6},{4,0},{6,2},{1,5},{3,7},{5,1},{7,3},{8,12},{10,14},{12... | collective-permute-start | bytes 589832 | tf_op jit(solution)/shard_map/ppermute | solution.py:369
  61.2 3.1 %collective-permute-start.9 = (bf16[192,512]{1,0:T(8,128)(2,1)S(1)}, bf16[192,512]{1,0:T(8,128)(2,1)S(1)}, u32[]{:S(2)}, u32[]{:S(2)}) collective-permute-start(bf16[192,512]{1,0:T(8,128)(2,1)S(1)} %get-tuple-element.24), channel_id=1, source_target_pairs={{0,6},{2,0},{4,2},{6,4},{1,7},{3,1},{5,3},{7,5},{8,14},{10,8},{12,... | collective-permute-start | bytes 589832 | tf_op jit(solution)/shard_map/ppermute | solution.py:369
  64.3 0.0 collective-permute-done.3.w1.refs_1_
  64.4 2.3 %collective-permute-start.4 = (bf16[160,512]{1,0:T(8,128)(2,1)S(1)}, bf16[160,512]{1,0:T(8,128)(2,1)S(1)}, u32[]{:S(2)}, u32[]{:S(2)}) collective-permute-start(bf16[160,512]{1,0:T(8,128)(2,1)S(1)} %slice.8), channel_id=1, source_target_pairs={{0,8},{8,16},{16,24},{24,0},{1,9},{9,17},{17,25},{25,1},{2,10},{10... | collective-permute-start | bytes 491528 | tf_op jit(solution)/shard_map/ppermute | solution.py:369
  66.7 0.0 copy-start.1
  66.7 4.9 %collective-permute-start.6 = (bf16[160,512]{1,0:T(8,128)(2,1)S(1)}, bf16[160,512]{1,0:T(8,128)(2,1)S(1)}, u32[]{:S(2)}, u32[]{:S(2)}) collective-permute-start(bf16[160,512]{1,0:T(8,128)(2,1)S(1)} %slice.9), channel_id=1, source_target_pairs={{0,24},{8,0},{16,8},{24,16},{1,25},{9,1},{17,9},{25,17},{2,26},{10... | collective-permute-start | bytes 491528 | tf_op jit(solution)/shard_map/ppermute | solution.py:369
  71.6 0.0 collective-permute-done.8.f2.refs_6_
  71.6 0.0 collective-permute-done.9.f3.refs_7_
  71.6 1.6 %collective-permute-done.4.w2a.refs_2_ = bf16[160,512]{1,0:T(8,128)(2,1)S(1)} collective-permute-done((bf16[160,512]{1,0:T(8,128)(2,1)S(1)}, bf16[160,512]{1,0:T(8,128)(2,1)S(1)}, u32[]{:S(2)}, u32[]{:S(2)}) %collective-permute-start.4) | collective-permute-done | bytes 163872 | tf_op jit(solution)/shard_map/ppermute | solution.py:369
  73.3 1.7 %collective-permute-done.6.w2b.refs_3_ = bf16[160,512]{1,0:T(8,128)(2,1)S(1)} collective-permute-done((bf16[160,512]{1,0:T(8,128)(2,1)S(1)}, bf16[160,512]{1,0:T(8,128)(2,1)S(1)}, u32[]{:S(2)}, u32[]{:S(2)}) %collective-permute-start.6) | collective-permute-done | bytes 163872 | tf_op jit(solution)/shard_map/ppermute | solution.py:369
  75.0 0.1 pack_for_core.1
  75.1 1.9 %collective-permute-start.10 = (bf16[1280,512]{1,0:T(8,128)(2,1)S(1)}, bf16[1280,512]{1,0:T(8,128)(2,1)S(1)}, u32[]{:S(2)}, u32[]{:S(2)}) collective-permute-start(bf16[1280,512]{1,0:T(8,128)(2,1)S(1)} %pack_for_core.1), channel_id=1, source_target_pairs={{0,1},{1,0},{2,3},{3,2},{4,5},{5,4},{6,7},{7,6},{8,9},{9,8},{10,11... | collective-permute-start | bytes 3932168 | tf_op jit(solution)/shard_map/ppermute | solution.py:373
  77.0 2.0 %project_own.1 = (f32[256,2048]{1,0:T(8,128)S(1)}, bf16[256,256]{1,0:T(8,128)(2,1)S(1)}, bf16[512,512]{1,0:T(8,128)(2,1)S(1)}, bf16[256,512]{1,0:T(8,128)(2,1)S(1)}) custom-call(s32[5]{0:T(128)S(1)} %copy-done.2, s32[1,256]{1,0:T(1,128)S(1)} %bitcast.11, bf16[256,512]{1,0:T(8,128)(2,1)S(1)} %bitcast.8, bf16[320,512]{1,0:T(8,128)(2,1)S(1)} %strip_ids.1.w0.refs_0_, ...), custom_call_target="tpu_custom_call" | custom-call | tf_op jit(solution)/shard_map/project_own/pallas_call | solution.py:258
  79.0 1.0 %collective-permute-done.10.other = bf16[1280,512]{1,0:T(8,128)(2,1)S(1)} collective-permute-done((bf16[1280,512]{1,0:T(8,128)(2,1)S(1)}, bf16[1280,512]{1,0:T(8,128)(2,1)S(1)}, u32[]{:S(2)}, u32[]{:S(2)}) %collective-permute-start.10) | collective-permute-done | bytes 1310752 | tf_op jit(solution)/shard_map/ppermute | solution.py:373
  80.0 1.6 %project.1 = (f32[256,512]{1,0:T(8,128)S(1)}, bf16[256,512]{1,0:T(8,128)(2,1)S(1)}, f32[256,512]{1,0:T(8,128)S(1)}, bf16[512,512]{1,0:T(8,128)(2,1)S(1)}) custom-call(s32[5]{0:T(128)S(1)} %copy-done.2, f32[256,2048]{1,0:T(8,128)S(1)} %get-tuple-element.25.part, bf16[256,256]{1,0:T(8,128)(2,1)S(1)} %get-tuple-element.26.rest, ...), custom_call_target="tpu_custom_call" | custom-call | flops 13400000512 | tf_op jit(solution)/shard_map/project/pallas_call | solution.py:302
  81.6 5.0 %all-to-all-done.hist = bf16[64,2,4,1024]{3,2,1,0:T(4,128)(2,1)S(1)} async-done(((bf16[64,2,4,1024]{3,2,1,0:T(4,128)(2,1)}), bf16[64,2,4,1024]{3,2,1,0:T(4,128)(2,1)S(1)}, u32[]{:S(2)}, u32[]{:S(2)}) %all-to-all-start) | async-done | bytes 1048608 | tf_op jit(solution)/shard_map/all_to_all | solution.py:404
  86.6 2.4 %score.1 = f32[2,128]{1,0:T(2,128)} custom-call(s32[2]{0:T(128)S(1)} %copy-done.4, bf16[64,2,4,1024]{3,2,1,0:T(4,128)(2,1)S(1)} %all-to-all-done.hist, bf16[256,512]{1,0:T(8,128)(2,1)S(1)} %get-tuple-element.28.query, f32[256,512]{1,0:T(8,128)S(1)} %get-tuple-element.29.self_term, f32[256,512]{1,0:T(8,128)S(1)} %get-tuple-element.30.gate, ...), custom_call_target="tpu_custom_call" | custom-call | tf_op jit(solution)/shard_map/score/pallas_call | solution.py:357
  (15 shorter events, 0.1 us)
Async XLA Ops:
  3.2 28.7 %copy-start.3 = (s32[2,128]{1,0:T(2,128)S(1)}, s32[2,128]{1,0:T(2,128)}, u32[]{:S(2)}) copy-start(s32[2,128]{1,0:T(2,128)} %param.14) | copy-start | bytes 3076
  3.2 28.8 %copy-start = (bf16[1024,512]{1,0:T(8,128)(2,1)S(1)}, bf16[1024,512]{1,0:T(8,128)(2,1)}, u32[]{:S(2)}) copy-start(bf16[1024,512]{1,0:T(8,128)(2,1)} %table.1) | copy-start | bytes 3145732
  3.2 28.7 %collective-permute-start = (bf16[40,512]{1,0:T(8,128)(2,1)}, bf16[40,512]{1,0:T(8,128)(2,1)S(1)}, u32[]{:S(2)}, u32[]{:S(2)}) collective-permute-start(bf16[40,512]{1,0:T(8,128)(2,1)} %get-tuple-element.20), channel_id=1, source_target_pairs={{0,0},{1,33},{2,66},{3,99},{4,132},{5,165},{6,198},{7,231},{32,32}... | collective-permute-start | bytes 122888 | tf_op jit(solution)/shard_map/ppermute | solution.py:392
  15.1 16.7 %collective-permute-start.1 = (bf16[40,512]{1,0:T(8,128)(2,1)}, bf16[40,512]{1,0:T(8,128)(2,1)S(1)}, u32[]{:S(2)}, u32[]{:S(2)}) collective-permute-start(bf16[40,512]{1,0:T(8,128)(2,1)} %get-tuple-element.20), channel_id=1, source_target_pairs={{0,256},{1,289},{2,322},{3,355},{4,388},{5,421},{6,454},{7,487},{3... | collective-permute-start | bytes 122888 | tf_op jit(solution)/shard_map/ppermute | solution.py:392
  17.9 68.7 %all-to-all-start = ((bf16[64,2,4,1024]{3,2,1,0:T(4,128)(2,1)}), bf16[64,2,4,1024]{3,2,1,0:T(4,128)(2,1)S(1)}, u32[]{:S(2)}, u32[]{:S(2)}) async-start(bf16[64,2,4,1024]{3,2,1,0:T(4,128)(2,1)} %get-tuple-element.19), calls=%async_computation | async-start | bytes 2097152 | tf_op jit(solution)/shard_map/all_to_all | solution.py:404
  32.1 21.6 %copy-start.2 = (s32[5]{0:T(128)S(1)}, s32[5]{0:T(128)}, u32[]{:S(2)}) copy-start(s32[5]{0:T(128)} %stack.23.place) | copy-start | bytes 64
  32.1 14.5 %collective-permute-start.2 = (bf16[1024,512]{1,0:T(8,128)(2,1)S(1)}, bf16[1024,512]{1,0:T(8,128)(2,1)S(1)}, u32[]{:S(2)}, u32[]{:S(2)}) collective-permute-start(bf16[1024,512]{1,0:T(8,128)(2,1)S(1)} %table_later.1), channel_id=1, source_target_pairs={{0,1},{1,0},{2,3},{3,2},{4,5},{5,4},{6,7},{7,6},{8,9},{9,8},{10,11... | collective-permute-start | bytes 3145736 | tf_op jit(solution)/shard_map/ppermute | solution.py:373
  46.7 17.7 %collective-permute-start.3 = (bf16[320,512]{1,0:T(8,128)(2,1)S(1)}, bf16[320,512]{1,0:T(8,128)(2,1)S(1)}, u32[]{:S(2)}, u32[]{:S(2)}) collective-permute-start(bf16[320,512]{1,0:T(8,128)(2,1)S(1)} %strip_ids.1.w0.refs_0_), channel_id=1, source_target_pairs={{0,8},{8,16},{16,24},{24,0},{1,9},{9,17},{17,25},{25,1},{2,10},{10... | collective-permute-start | bytes 983048 | tf_op jit(solution)/shard_map/ppermute | solution.py:369
  50.1 16.5 %collective-permute-start.5 = (bf16[320,512]{1,0:T(8,128)(2,1)S(1)}, bf16[320,512]{1,0:T(8,128)(2,1)S(1)}, u32[]{:S(2)}, u32[]{:S(2)}) collective-permute-start(bf16[320,512]{1,0:T(8,128)(2,1)S(1)} %strip_ids.1.w0.refs_0_), channel_id=1, source_target_pairs={{0,24},{8,0},{16,8},{24,16},{1,25},{9,1},{17,9},{25,17},{2,26},{10... | collective-permute-start | bytes 983048 | tf_op jit(solution)/shard_map/ppermute | solution.py:369
  55.7 15.9 %collective-permute-start.7 = (bf16[192,512]{1,0:T(8,128)(2,1)S(1)}, bf16[192,512]{1,0:T(8,128)(2,1)S(1)}, u32[]{:S(2)}, u32[]{:S(2)}) collective-permute-start(bf16[192,512]{1,0:T(8,128)(2,1)S(1)} %get-tuple-element.22), channel_id=1, source_target_pairs={{0,2},{2,4},{4,6},{6,0},{1,3},{3,5},{5,7},{7,1},{8,10},{10,12},{12... | collective-permute-start | bytes 589832 | tf_op jit(solution)/shard_map/ppermute | solution.py:369
  58.4 13.2 %collective-permute-start.8 = (bf16[192,512]{1,0:T(8,128)(2,1)S(1)}, bf16[192,512]{1,0:T(8,128)(2,1)S(1)}, u32[]{:S(2)}, u32[]{:S(2)}) collective-permute-start(bf16[192,512]{1,0:T(8,128)(2,1)S(1)} %get-tuple-element.23), channel_id=1, source_target_pairs={{0,4},{2,6},{4,0},{6,2},{1,5},{3,7},{5,1},{7,3},{8,12},{10,14},{12... | collective-permute-start | bytes 589832 | tf_op jit(solution)/shard_map/ppermute | solution.py:369
  61.2 10.4 %collective-permute-start.9 = (bf16[192,512]{1,0:T(8,128)(2,1)S(1)}, bf16[192,512]{1,0:T(8,128)(2,1)S(1)}, u32[]{:S(2)}, u32[]{:S(2)}) collective-permute-start(bf16[192,512]{1,0:T(8,128)(2,1)S(1)} %get-tuple-element.24), channel_id=1, source_target_pairs={{0,6},{2,0},{4,2},{6,4},{1,7},{3,1},{5,3},{7,5},{8,14},{10,8},{12,... | collective-permute-start | bytes 589832 | tf_op jit(solution)/shard_map/ppermute | solution.py:369
  64.4 8.9 %collective-permute-start.4 = (bf16[160,512]{1,0:T(8,128)(2,1)S(1)}, bf16[160,512]{1,0:T(8,128)(2,1)S(1)}, u32[]{:S(2)}, u32[]{:S(2)}) collective-permute-start(bf16[160,512]{1,0:T(8,128)(2,1)S(1)} %slice.8), channel_id=1, source_target_pairs={{0,8},{8,16},{16,24},{24,0},{1,9},{9,17},{17,25},{25,1},{2,10},{10... | collective-permute-start | bytes 491528 | tf_op jit(solution)/shard_map/ppermute | solution.py:369
  66.7 10.3 %copy-start.1 = (bf16[2,128,512]{2,1,0:T(8,128)(2,1)S(1)}, bf16[2,128,512]{2,1,0:T(8,128)(2,1)}, u32[]{:S(2)}) copy-start(bf16[2,128,512]{2,1,0:T(8,128)(2,1)} %param.8) | copy-start | bytes 786436
  66.7 8.3 %collective-permute-start.6 = (bf16[160,512]{1,0:T(8,128)(2,1)S(1)}, bf16[160,512]{1,0:T(8,128)(2,1)S(1)}, u32[]{:S(2)}, u32[]{:S(2)}) collective-permute-start(bf16[160,512]{1,0:T(8,128)(2,1)S(1)} %slice.9), channel_id=1, source_target_pairs={{0,24},{8,0},{16,8},{24,16},{1,25},{9,1},{17,9},{25,17},{2,26},{10... | collective-permute-start | bytes 491528 | tf_op jit(solution)/shard_map/ppermute | solution.py:369
  75.1 4.9 %collective-permute-start.10 = (bf16[1280,512]{1,0:T(8,128)(2,1)S(1)}, bf16[1280,512]{1,0:T(8,128)(2,1)S(1)}, u32[]{:S(2)}, u32[]{:S(2)}) collective-permute-start(bf16[1280,512]{1,0:T(8,128)(2,1)S(1)} %pack_for_core.1), channel_id=1, source_target_pairs={{0,1},{1,0},{2,3},{3,2},{4,5},{5,4},{6,7},{7,6},{8,9},{9,8},{10,11... | collective-permute-start | bytes 3932168 | tf_op jit(solution)/shard_map/ppermute | solution.py:373
  80.0 6.6 %copy-start.4 = (s32[2]{0:T(128)S(1)}, s32[2]{0:T(128)}, u32[]{:S(2)}) copy-start(s32[2]{0:T(128)} %lengths.1) | copy-start | bytes 28
